TPU v7x, 512 devices: a whole 4x8x8 slice. The times are simulated.
512 devices in a mesh: seq: 8 (over x, core), exp: 64 (over y, z).
Axes of the slice: x: 4, y: 8, z: 8, core: 2. Of those that a mesh axis runs over, the one named last changes fastest.
Arguments:
- hidden: bfloat16 [65536, 1024], P(('seq', 'exp')), may hold values from -6 to 6
- queries: bfloat16 [65536, 1024], P(('seq', 'exp')), may hold values from -16 to 16
- thinker_keys: bfloat16 [4096, 128], P(('seq', 'exp')), may hold values from -16 to 16
- thinker_values: bfloat16 [4096, 128], P(('seq', 'exp')), may hold values from -15 to 15
- thinker_lengths: int32 [2048], P(('seq', 'exp')), may hold values from 1 to 8, 4096 in all
- out_proj: bfloat16 [1024, 1024], replicated, may hold values from -0.1875 to 0.1875
- expert_ids: int32 [65536, 4], P(('seq', 'exp')), may hold values from 0 to 63, all different within a row; in each aligned block of 128 rows (0 to 127, 128 to 255, ...) at most 10 rows name the same one
- gate_values: bfloat16 [65536, 4], P(('seq', 'exp')), may hold values from 0.099609375 to 1
- w_gate: bfloat16 [64, 1024, 768], P('exp', 'seq'), may hold values from -0.1875 to 0.1875
- w_up: bfloat16 [64, 1024, 768], P('exp', 'seq'), may hold values from -0.1875 to 0.1875
- w_down: bfloat16 [64, 768, 1024], P('exp', None, 'seq'), may hold values from -0.21875 to 0.21875
- cotangent: bfloat16 [65536, 1024], P(('seq', 'exp')), may hold values from -2.5 to 2.5
Outputs:
- grad_input: float32 [65536, 1024], P(('seq', 'exp'))
- grad_gates: bfloat16 [65536, 4], P(('seq', 'exp'))
Inputs may be any that keep to these rules, and one draw needn't show every extreme that they name: `thinker_lengths`: each talker group of 32 tokens brings at least one thinker row, the groups of the dialogue together bring 4096, and some group brings exactly 8. `expert_ids`: the 4 experts of a token differ. Among the routes of the 128 tokens of one device no expert is named more than 10 times, and in every draw some expert is named exactly 10 times by the tokens of some device.
All inputs are finite; a program needn't handle non-finite values.
Results may differ from a plain program's by a relative error of at most 0.014.
Values may be sent and summed in bfloat16 or wider, within the bound.
No kernel may reach another device: no remote copies, remote signals or barrier semaphores. Data moves between devices by JAX's collectives and lax.ppermute only.
A program may use at most 64 MiB of HBM per device.

v0:
```python
import jax
import jax.numpy as jnp
from jax import lax
from jax.sharding import PartitionSpec as P

GROUP = 32


NEG_FILL = -1e30


def carried_in(part, axis, combine, identity):
    place = lax.axis_index(axis)
    gathered = lax.all_gather(part, axis)
    state = jnp.zeros_like(part) + jnp.asarray(identity, part.dtype)

    def one(turn, state):
        return combine(state, lax.dynamic_index_in_dim(gathered, turn, 0, False))

    return lax.fori_loop(0, place, one, state)


def contract_last(left, right):
    return lax.dot_general(
        left, right, (((1,), (1,)), ((), ())), preferred_element_type=jnp.float32
    )


def group_attend(running, pieces, q_heads, limits, score_scale):
    key_all, value_all = pieces
    row_count = key_all.shape[0]
    block_rows = 512
    block_count = row_count // block_rows

    def one_block(fold_state, block_index):
        run_max, run_sum, acc_values = fold_state
        key_block = lax.dynamic_slice_in_dim(key_all, block_index * block_rows, block_rows, 0)
        value_block = lax.dynamic_slice_in_dim(value_all, block_index * block_rows, block_rows, 0)
        scores = (
            jnp.einsum("thd,jd->thj", q_heads, key_block, preferred_element_type=jnp.float32)
            * score_scale
        )
        positions = block_index * block_rows + jnp.arange(block_rows, dtype=jnp.int32)
        is_valid = positions[None, None, :] < limits[:, None, None]
        scores = jnp.where(is_valid, scores, NEG_FILL)
        new_max = jnp.maximum(run_max, jnp.max(scores, axis=2))
        weights = jnp.where(is_valid, jnp.exp(scores - new_max[:, :, None]), 0.0)
        factor = jnp.exp(run_max - new_max)
        run_sum = run_sum * factor + jnp.sum(weights, axis=2)
        acc_values = acc_values * factor[:, :, None] + jnp.einsum(
            "thj,jd->thd",
            weights.astype(jnp.bfloat16),
            value_block,
            preferred_element_type=jnp.float32,
        )
        return ((new_max, run_sum, acc_values), None)

    fold_state, unused = lax.scan(one_block, running, jnp.arange(block_count))
    return fold_state


def local(
    hidden,
    queries,
    thinker_keys,
    thinker_values,
    thinker_lengths,
    out_proj,
    expert_ids,
    gate_values,
    w_gate,
    w_up,
    w_down,
    cotangent,
):
    tok_rows, model_width = hidden.shape
    head_dim = thinker_keys.shape[1]
    head_count = queries.shape[1] // head_dim
    top_count = expert_ids.shape[1]
    experts = lax.axis_size("exp")
    capacity = tok_rows * top_count * 5 // (4 * experts)
    slots = experts * capacity
    local_total = jnp.sum(thinker_lengths)
    offset = carried_in(
        local_total, ("seq", "exp"), lambda earlier, later: earlier + later, jnp.int32(0)
    )
    group_ends = offset + jnp.cumsum(thinker_lengths)
    limits = jnp.repeat(group_ends, GROUP, total_repeat_length=tok_rows)
    q_heads = queries.reshape(tok_rows, head_count, head_dim)
    score_scale = head_dim ** (-0.5)
    start_state = (
        jnp.full((tok_rows, head_count), NEG_FILL, jnp.float32),
        jnp.zeros((tok_rows, head_count), jnp.float32),
        jnp.zeros((tok_rows, head_count, head_dim), jnp.float32),
    )
    key_all, value_all = (
        lax.all_gather(thinker_keys, ("seq", "exp"), axis=0, tiled=True),
        lax.all_gather(thinker_values, ("seq", "exp"), axis=0, tiled=True),
    )
    run_max, run_sum, acc_values = group_attend(
        start_state, (key_all, value_all), q_heads, limits, score_scale
    )
    attended = (
        (acc_values / run_sum[:, :, None])
        .astype(jnp.bfloat16)
        .reshape(tok_rows, head_count * head_dim)
    )
    mixed = (
        hidden.astype(jnp.float32) + jnp.dot(attended, out_proj, preferred_element_type=jnp.float32)
    ).astype(jnp.bfloat16)
    flat_ids = expert_ids.reshape(-1)
    routes = flat_ids.shape[0]
    onehot = (flat_ids[:, None] == jnp.arange(experts, dtype=jnp.int32)[None, :]).astype(jnp.int32)
    slot_rank = jnp.sum((jnp.cumsum(onehot, axis=0) - onehot) * onehot, axis=1)
    slot_index = flat_ids * capacity + slot_rank
    source = (
        jnp.full((slots,), -1, jnp.int32).at[slot_index].set(jnp.arange(routes, dtype=jnp.int32))
    )
    filled = source >= 0
    route_safe = jnp.where(filled, source, 0)
    token_safe = route_safe // top_count
    send_rows = jnp.where(filled[:, None], mixed[token_safe], jnp.zeros((), jnp.bfloat16)).reshape(
        experts, capacity, model_width
    )
    send_cot = jnp.where(
        filled[:, None], cotangent[token_safe], jnp.zeros((), jnp.bfloat16)
    ).reshape(experts, capacity, model_width)
    send_gate = jnp.where(
        filled, gate_values.reshape(-1)[route_safe], jnp.zeros((), jnp.bfloat16)
    ).reshape(experts, capacity)
    recv_rows = lax.all_to_all(send_rows, "exp", split_axis=0, concat_axis=0, tiled=True)
    slot_rows = recv_rows.reshape(slots, model_width)
    gate_full, up_full = (
        lax.all_gather(w_gate[0], "seq", axis=0, tiled=True),
        lax.all_gather(w_up[0], "seq", axis=0, tiled=True),
    )
    down_full = lax.all_gather(w_down[0], "seq", axis=1, tiled=True)
    gate_lin = jnp.dot(slot_rows, gate_full, preferred_element_type=jnp.float32)
    up_lin = jnp.dot(slot_rows, up_full, preferred_element_type=jnp.float32)
    recv_cot, recv_gate = (
        lax.all_to_all(send_cot, "exp", split_axis=0, concat_axis=0, tiled=True),
        lax.all_to_all(send_gate, "exp", split_axis=0, concat_axis=0, tiled=True),
    )
    cot_rows = recv_cot.reshape(slots, model_width)
    gates_in = recv_gate.reshape(slots).astype(jnp.float32)
    down_back = contract_last(cot_rows, down_full)
    sigmoid_gate = jax.nn.sigmoid(gate_lin)
    swish_gate = gate_lin * sigmoid_gate
    activation = swish_gate * up_lin
    gate_grad = jnp.sum(activation * down_back, axis=1).astype(jnp.bfloat16)
    act_grad = gates_in[:, None] * down_back
    gate_back = (act_grad * up_lin * sigmoid_gate * (1.0 + gate_lin * (1.0 - sigmoid_gate))).astype(
        jnp.bfloat16
    )
    up_back = (act_grad * swish_gate).astype(jnp.bfloat16)
    route_sum = contract_last(gate_back, gate_full) + contract_last(up_back, up_full)
    route_grad = route_sum.astype(jnp.bfloat16)
    back_rows, back_gate = (
        lax.all_to_all(
            route_grad.reshape(experts, capacity, model_width),
            "exp",
            split_axis=0,
            concat_axis=0,
            tiled=True,
        ),
        lax.all_to_all(
            gate_grad.reshape(experts, capacity), "exp", split_axis=0, concat_axis=0, tiled=True
        ),
    )
    picked = (
        back_rows.reshape(slots, model_width)[slot_index]
        .astype(jnp.float32)
        .reshape(tok_rows, top_count, model_width)
    )
    grad_input = jnp.sum(picked, axis=1)
    grad_gates = back_gate.reshape(slots)[slot_index].reshape(tok_rows, top_count)
    return (grad_input, grad_gates)


def solution(mesh):
    return jax.shard_map(
        local,
        mesh=mesh,
        in_specs=(
            P(("seq", "exp"), None),
            P(("seq", "exp"), None),
            P(("seq", "exp"), None),
            P(("seq", "exp"), None),
            P(("seq", "exp")),
            P(),
            P(("seq", "exp"), None),
            P(("seq", "exp"), None),
            P("exp", "seq", None),
            P("exp", "seq", None),
            P("exp", None, "seq"),
            P(("seq", "exp"), None),
        ),
        out_specs=(P(("seq", "exp"), None), P(("seq", "exp"), None)),
        check_vma=False,
    )
```

profile of v0, /device:TPU:31, one launch (start us, length us, event | category | flops | bytes accessed | tf_op | source)
XLA Modules:
  0.0 1142.9 jit_solution(9779873937164692926)
XLA Ops:
  15.7 4.3 gather_fusion
  20.8 15.8 %all-to-all-start = ((bf16[64,1,10]{2,1,0:T(2,128)(2,1)}), bf16[64,1,10]{2,1,0:T(2,128)(2,1)S(1)}, u32[]{:S(2)}, u32[]{:S(2)}) async-start(bf16[64,1,10]{2,1,0:T(2,128)(2,1)} %all_to_all.25), calls=%async_computation | async-start | bytes 65536 | tf_op jit(solution)/shard_map/all_to_all | solution.py:142
  39.0 96.7 %all-reduce = s32[512]{0:T(512)S(1)} all-reduce(s32[512]{0:T(512)S(1)} %dynamic-update-slice.3), channel_id=1, replica_groups=mesh['seq'=8,'exp'=64] {'seq','exp'}, use_global_device_ids=true, to_apply=%add | all-reduce | flops 512 | bytes 4096
  135.7 654.8 %while.26 = (s32[]{:T(128)}, s32[]{:T(128)}, s32[]{:T(128)}, s32[512]{0:T(512)S(1)}, s32[]{:T(128)}, /*index=5*/s32[]{:T(128)}, s32[]{:T(128)}) while((s32[]{:T(128)}, s32[]{:T(128)}, s32[]{:T(128)}, s32[512]{0:T(512)S(1)}, s32[]{:T(128)}, /*index=5*/s32[]{:T(128)}, s32[]{:T(128)}) %tuple.59), condition=%wide.region_6.7_spmd, body=%wide.region_5.6_spmd.sunk | while | flops 6 | bytes 135 | solution.py:20
  792.7 3.5 gather_fusion.1
  796.1 3.6 gather.25
  799.8 86.3 %while.27 = (s32[]{:T(128)}, f32[128,8]{0,1:T(8,128)S(1)}, f32[128,8]{0,1:T(8,128)S(1)}, f32[128,8,128]{2,0,1:T(8,128)S(1)}, s32[8]{0:T(128)S(1)}, /*index=5*/bf...) while((s32[]{:T(128)}, f32[128,8]{0,1:T(8,128)S(1)}, ...), condition=%wide.region_11.12_spmd.clone, body=%wide.region_8.11_spmd.clone.sunk | while | flops 275715968 | bytes 16586411 | solution.py:58
  803.9 2.7 fusion.61
  814.6 2.7 fusion.61
  825.4 2.7 fusion.61
  836.2 2.7 fusion.61
  847.0 2.7 fusion.61
  868.6 2.7 fusion.61
  887.5 3.5 gather_fusion.2
  891.0 3.6 gather.28
  894.6 4.5 broadcast_select_fusion.1
  899.1 58.4 %all-to-all-start.2 = ((bf16[64,10,1024]{2,1,0:T(8,128)(2,1)}), bf16[64,10,1024]{2,1,0:T(8,128)(2,1)}, u32[]{:S(2)}, u32[]{:S(2)}) async-start(bf16[64,10,1024]{2,1,0:T(8,128)(2,1)} %get-tuple-element.200), calls=%async_computation.2 | async-start | bytes 4194304 | tf_op jit(solution)/shard_map/all_to_all | solution.py:131
  958.1 30.2 %all-to-all-done.2 = bf16[64,10,1024]{2,1,0:T(8,128)(2,1)} async-done(((bf16[64,10,1024]{2,1,0:T(8,128)(2,1)}), bf16[64,10,1024]{2,1,0:T(8,128)(2,1)}, u32[]{:S(2)}, u32[]{:S(2)}) %all-to-all-start.2) | async-done | bytes 1310752 | tf_op jit(solution)/shard_map/all_to_all | solution.py:131
  988.3 6.3 all-to-all-start.1
  995.4 3.6 reshape.229
  999.1 26.3 %all-to-all-done.1 = bf16[64,10,1024]{2,1,0:T(8,128)(2,1)} async-done(((bf16[64,10,1024]{2,1,0:T(8,128)(2,1)}), bf16[64,10,1024]{2,1,0:T(8,128)(2,1)}, u32[]{:S(2)}, u32[]{:S(2)}) %all-to-all-start.1) | async-done | bytes 1310752 | tf_op jit(solution)/shard_map/all_to_all | solution.py:141
  1028.0 4.3 fusion.24
  1032.2 4.3 fusion.27
  1036.5 5.2 multiply_reduce_fusion
  1042.5 6.1 all-to-all-start.4
  1048.7 5.0 fusion.22
  1057.0 11.8 %all-to-all-start.3 = ((bf16[64,10,1024]{2,1,0:T(8,128)(2,1)}), bf16[64,10,1024]{2,1,0:T(8,128)(2,1)}, u32[]{:S(2)}, u32[]{:S(2)}) async-start(bf16[64,10,1024]{2,1,0:T(8,128)(2,1)} %reshape.230), calls=%async_computation.3 | async-start | bytes 4194304 | tf_op jit(solution)/shard_map/all_to_all | solution.py:159
  1069.1 3.5 gather_fusion.4
  1073.4 51.3 %all-to-all-done.3 = bf16[64,10,1024]{2,1,0:T(8,128)(2,1)} async-done(((bf16[64,10,1024]{2,1,0:T(8,128)(2,1)}), bf16[64,10,1024]{2,1,0:T(8,128)(2,1)}, u32[]{:S(2)}, u32[]{:S(2)}) %all-to-all-start.3) | async-done | bytes 1310752 | tf_op jit(solution)/shard_map/all_to_all | solution.py:159
  1127.2 2.8 gather_fusion.3
  1130.0 2.7 reshape.235
  1132.8 3.7 reduce_sum.50
  (650 shorter events, 406.1 us)
Async XLA Ops:
  7.2 879.2 %copy-start = (bf16[1024,1024]{1,0:T(8,128)(2,1)S(1)}, bf16[1024,1024]{1,0:T(8,128)(2,1)}, u32[]{:S(2)}) copy-start(bf16[1024,1024]{1,0:T(8,128)(2,1)} %param.23) | copy-start | bytes 6291460
  7.2 30.4 %copy-start.8 = (s32[4]{0:T(128)S(1)}, s32[4]{0:T(128)}, u32[]{:S(2)}) copy-start(s32[4]{0:T(128)} %param.22) | copy-start | bytes 52
  7.2 792.6 %all-gather.11.cloned.1.call-start = ((), (), s32[]{:S(2)}) async-start(), calls=%async_computation.6 | async-start | bytes 1050624 | tf_op jit(solution)/shard_map/all_gather | solution.py:98
  7.9 791.8 %all-gather.9.cloned.1.call-start = ((), (), s32[]{:S(2)}) async-start(), calls=%async_computation.5 | async-start | bytes 1050624 | tf_op jit(solution)/shard_map/all_gather | solution.py:97
  13.0 779.6 %copy-start.1 = (bf16[128,1024]{1,0:T(8,128)(2,1)S(1)}, bf16[128,1024]{1,0:T(8,128)(2,1)}, u32[]{:S(2)}) copy-start(bf16[128,1024]{1,0:T(8,128)(2,1)} %param.29) | copy-start | bytes 786436
  20.8 878.4 %all-to-all-start = ((bf16[64,1,10]{2,1,0:T(2,128)(2,1)}), bf16[64,1,10]{2,1,0:T(2,128)(2,1)S(1)}, u32[]{:S(2)}, u32[]{:S(2)}) async-start(bf16[64,1,10]{2,1,0:T(2,128)(2,1)} %all_to_all.25), calls=%async_computation | async-start | bytes 65536 | tf_op jit(solution)/shard_map/all_to_all | solution.py:142
  36.6 991.3 %all-gather.17.cloned.1.call-start = ((), (), s32[]{:S(2)}) async-start(), calls=%async_computation.9 | async-start | bytes 1769472 | tf_op jit(solution)/shard_map/all_gather | solution.py:134
  796.1 3.6 copy-start.4
  796.1 3.6 copy-start.5
  796.1 3.6 copy-start.6
  806.5 2.3 copy-start.2
  817.3 2.3 copy-start.2
  828.1 2.3 copy-start.2
  838.9 2.3 copy-start.2
  849.7 2.3 copy-start.2
  860.5 2.3 copy-start.2
  871.2 2.3 copy-start.2
  882.0 2.3 copy-start.2
  886.1 1.0 copy-start.3
  899.1 89.2 %all-to-all-start.2 = ((bf16[64,10,1024]{2,1,0:T(8,128)(2,1)}), bf16[64,10,1024]{2,1,0:T(8,128)(2,1)}, u32[]{:S(2)}, u32[]{:S(2)}) async-start(bf16[64,10,1024]{2,1,0:T(8,128)(2,1)} %get-tuple-element.200), calls=%async_computation.2 | async-start | bytes 4194304 | tf_op jit(solution)/shard_map/all_to_all | solution.py:131
  957.6 74.7 %all-gather.15.cloned.1.call-start = ((), (), s32[]{:S(2)}) async-start(), calls=%async_computation.8 | async-start | bytes 1769472 | tf_op jit(solution)/shard_map/all_gather | solution.py:135
  988.3 37.0 %all-to-all-start.1 = ((bf16[64,10,1024]{2,1,0:T(8,128)(2,1)}), bf16[64,10,1024]{2,1,0:T(8,128)(2,1)}, u32[]{:S(2)}, u32[]{:S(2)}) async-start(bf16[64,10,1024]{2,1,0:T(8,128)(2,1)} %get-tuple-element.199), calls=%async_computation.1 | async-start | bytes 4194304 | tf_op jit(solution)/shard_map/all_to_all | solution.py:141
  994.6 41.9 %all-gather.13.cloned.1.call-start = ((), (), s32[]{:S(2)}) async-start(), calls=%async_computation.7 | async-start | bytes 1769472 | tf_op jit(solution)/shard_map/all_gather | solution.py:137
  1042.5 14.5 %all-to-all-start.4 = ((bf16[64,1,10]{2,1,0:T(2,128)(2,1)}), bf16[64,1,10]{2,1,0:T(2,128)(2,1)S(1)}, u32[]{:S(2)}, u32[]{:S(2)}) async-start(bf16[64,1,10]{2,1,0:T(2,128)(2,1)} %convert_element_type.76), calls=%async_computation.4 | async-start | bytes 65536 | tf_op jit(solution)/shard_map/all_to_all | solution.py:166
  1048.6 5.0 copy-start.7
  1048.6 5.0 copy-start.9
  1048.7 5.0 copy-start.10
  1057.0 67.7 %all-to-all-start.3 = ((bf16[64,10,1024]{2,1,0:T(8,128)(2,1)}), bf16[64,10,1024]{2,1,0:T(8,128)(2,1)}, u32[]{:S(2)}, u32[]{:S(2)}) async-start(bf16[64,10,1024]{2,1,0:T(8,128)(2,1)} %reshape.230), calls=%async_computation.3 | async-start | bytes 4194304 | tf_op jit(solution)/shard_map/all_to_all | solution.py:159
Sparse Core Ops, SparseCore 0:
  12.2 115.7 all-gather.10
  132.2 109.8 all-gather.8
  244.2 26.9 all-gather.16
  960.2 28.4 all-gather.14
  997.2 30.0 all-gather.12
where the time goes:
time: 1150 us; the launch traced here: 1140 us
  local copies, waits for them, and re-layouts  369 us (32%)
  loops' own time  346 us (30%)
  waiting for transfers between devices  111 us (10%)
  starting transfers between devices  98.7 us (9%)
  blocking collectives  96.7 us (8%)
  matrix products  55.9 us (5%)
  other arithmetic  51.6 us (4%)
  between operations  14.2 us (1%)
    another operation x1, loops' own time, carried_in(): return lax.fori_loop(0, place, one, state)  340 us
    dynamic_slice x472, local copies, waits for them, and re-layouts, one(): return combine(state, lax.dynamic_index_in_dim(gathered, turn, 0, False))  315 us
    unnamed x1, blocking collectives  96.7 us
    all_to_all x1, starting transfers between devices, local(): lax.all_to_all(send_rows, 'exp', split_axis=0, concat_axis=0, tiled=True)  58.4 us
    all_to_all x1, waiting for transfers between devices, local(): lax.all_to_all(route_grad.reshape(experts, capacity, model_width), 'exp',...  51.3 us
    all_to_all x1, waiting for transfers between devices, local(): lax.all_to_all(send_rows, 'exp', split_axis=0, concat_axis=0, tiled=True)  30.2 us
    all_to_all x1, waiting for transfers between devices, local(): lax.all_to_all(send_cot, 'exp', split_axis=0, concat_axis=0, tiled=True)  26.3 us
  transfers between devices with their start and end apart: 10, of which 4 were waited for; matrix products, arithmetic and copies ran while one was open for 40% of the time, Pallas kernels for 0%

commit v1 on v0

v1 whole, which is shorter than its diff:
```python
import functools

import jax
import jax.numpy as jnp
from jax import lax
from jax.experimental import pallas as pl
from jax.experimental.pallas import tpu as pltpu
from jax.sharding import PartitionSpec as P

GROUP = 32
NEG = -1e30
LANES = 128
F32 = jnp.float32
BF16 = jnp.bfloat16
MIB = 1 << 20


def params(mib):
    return pltpu.CompilerParams(vmem_limit_bytes=mib * MIB)


def vmem(count):
    return [pl.BlockSpec(memory_space=pltpu.VMEM)] * count


SMEM = pl.BlockSpec(memory_space=pltpu.SMEM)


def iota(shape, dim):
    return lax.broadcasted_iota(jnp.int32, shape, dim)


def dot(a, b, dims=((1,), (0,))):
    return lax.dot_general(a, b, (dims, ((), ())), preferred_element_type=F32)


def as_bf16(mask):
    return jnp.where(mask, 1.0, 0.0).astype(BF16)


def fold_matrix(slots, chunks):
    rows = slots * chunks
    row, col = iota((rows, rows), 0), iota((rows, rows), 1)
    return as_bf16((row // chunks) + (row % chunks) * slots == col)


def unfold_matrix(slots, chunks):
    rows = slots * chunks
    row, col = iota((rows, rows), 0), iota((rows, rows), 1)
    return as_bf16((col // chunks) + (col % chunks) * slots == row)


BLOCK = 32


def fold_rows(wide, matrix, store):
    chunks = wide.shape[1] // LANES
    size = BLOCK * chunks

    def stacked(b):
        part = wide[b * BLOCK : (b + 1) * BLOCK, :]
        return jnp.concatenate(
            [part[:, c * LANES : (c + 1) * LANES] for c in range(chunks)], axis=0
        )

    for b in range(0, wide.shape[0] // BLOCK, 2):
        two = jnp.concatenate([stacked(b), stacked(b + 1)], axis=1)
        out = dot(matrix, two).astype(BF16)
        store(b * size, out[:, :LANES])
        store((b + 1) * size, out[:, LANES:])


def unfold_rows(load, slots, chunks, matrix, ref):
    size = BLOCK * chunks
    for b in range(0, slots // BLOCK, 2):
        two = jnp.concatenate([load(b * size, size), load((b + 1) * size, size)], axis=1)
        out = dot(matrix, two).astype(BF16)
        for half in range(2):
            for c in range(chunks):
                ref[
                    (b + half) * BLOCK : (b + half + 1) * BLOCK, c * LANES : (c + 1) * LANES
                ] = out[c * BLOCK : (c + 1) * BLOCK, half * LANES : (half + 1) * LANES]


def pack_kernel(lens_ref, key_ref, value_ref, out_ref):
    copies = out_ref.shape[0]
    total = lens_ref[0]
    for i in range(1, lens_ref.shape[0]):
        total = total + lens_ref[i]
    rows = key_ref.shape[0]
    tot = jnp.full((rows, LANES), total.astype(F32), F32).astype(BF16)
    one = jnp.concatenate([key_ref[...], value_ref[...], tot], axis=1)
    out_ref[...] = jnp.broadcast_to(one[None], (copies,) + one.shape)


def segment_kernel(in_ref, out_ref, *, rows):
    count = in_ref.shape[0]
    out_ref[0:count, :] = in_ref[:, 0 : 2 * LANES]
    tot = in_ref[:, 2 * LANES :].astype(F32)
    row, lane = iota(tot.shape, 0), iota(tot.shape, 1)
    line = jnp.sum(jnp.where(row == lane * rows, tot, 0.0), axis=0, keepdims=True)
    more = out_ref.shape[0] - count
    line = jnp.broadcast_to(line, (more, LANES))
    out_ref[count:, :] = jnp.concatenate([line, jnp.zeros_like(line)], axis=1).astype(BF16)


def placed(slot_rows, top, slots, values=None):
    tokens = slot_rows.shape[1]
    place = iota((slots, tokens), 0)
    out = jnp.zeros((slots, tokens), F32)
    for k in range(top):
        value = 1.0 if values is None else values[k : k + 1, :]
        out = jnp.where(place == slot_rows[k : k + 1, :], value, out)
    return out.astype(BF16)


def dispatch_kernel(ids_ref, gate_ref, cot_ref, slot_ref, send_ref, *, experts, capacity):
    top, tokens = ids_ref.shape
    ids = ids_ref[...]
    expert = iota((experts, tokens), 0)
    named = jnp.zeros((experts, tokens), F32)
    for k in range(top):
        named = jnp.where(expert == ids[k : k + 1, :], 1.0, named)
    earlier = as_bf16(iota((tokens, tokens), 0) < iota((tokens, tokens), 1))
    before = dot(named.astype(BF16), earlier)
    slot_rows, ranks = [], []
    for k in range(top):
        own = ids[k : k + 1, :]
        rank = jnp.sum(jnp.where(expert == own, before, 0.0), axis=0, keepdims=True)
        rank = rank.astype(jnp.int32)
        ranks.append(rank)
        slot_rows.append(own * capacity + rank)
    both = jnp.concatenate(slot_rows + ranks, axis=0)
    slot_ref[...] = both
    slots = experts * capacity
    spread = placed(both, top, slots, gate_ref[...].astype(F32))
    wide = dot(spread, cot_ref[...]).astype(BF16)
    chunks = cot_ref.shape[1] // LANES

    def store(first, rows):
        send_ref[first : first + rows.shape[0], :] = rows

    fold_rows(wide, fold_matrix(BLOCK, chunks), store)


def attend_kernel(
    place_ref,
    lens_ref,
    kv_ref,
    query_ref,
    hidden_ref,
    proj_ref,
    slot_ref,
    send_ref,
    max_ref,
    acc_ref,
    *,
    segments,
    rows,
    pitch,
    top,
):
    tokens = query_ref.shape[0]
    heads = query_ref.shape[1] // LANES
    seq, exp = place_ref[0], place_ref[1]
    total = jnp.zeros((16, LANES), F32)
    lane = iota((16, LANES), 1)
    for s in range(segments):
        line = kv_ref[s * pitch + rows : s * pitch + rows + 16, 0:LANES].astype(F32)
        take = jnp.logical_or(seq > s, jnp.logical_and(seq == s, lane < exp))
        total = total + jnp.where(take, line, 0.0)
    offset = (jnp.sum(total) * (1.0 / 16.0)).astype(jnp.int32)
    ends = []
    for g in range(lens_ref.shape[0]):
        offset = offset + lens_ref[g]
        ends.append(offset)
    group = iota((tokens, 1), 0) // GROUP
    limits = jnp.zeros((tokens, 1), jnp.int32)
    for g, end in enumerate(ends):
        limits = jnp.where(group == g, end, limits)
    scale = LANES**-0.5 * 1.4426950408889634
    max_ref[...] = jnp.full(max_ref.shape, NEG, F32)
    acc_ref[...] = jnp.zeros(acc_ref.shape, F32)
    ones = as_bf16(iota((rows, LANES), 1) == 0)

    def block(masked):
        def body(b, carry):
            first = pl.multiple_of(b * pitch, 16)
            keys = kv_ref[pl.ds(first, rows), 0:LANES]
            values = kv_ref[pl.ds(first, rows), LANES : 2 * LANES]
            wide = jnp.concatenate([values, ones], axis=1)
            for h in range(heads):
                q = query_ref[:, h * LANES : (h + 1) * LANES]
                s = dot(q, keys, ((1,), (1,)))
                if masked:
                    seen = iota((tokens, rows), 1) + b * rows < limits
                    s = jnp.where(seen, s, NEG)
                old = max_ref[h]
                new = jnp.maximum(old, jnp.max(s, axis=1, keepdims=True))
                max_ref[h] = new
                w = jnp.exp2((s - new) * scale).astype(BF16)
                factor = jnp.exp2((old - new) * scale)
                acc_ref[h] = acc_ref[h] * factor + dot(w, wide)
            return carry

        return body

    full = ends[0] // rows
    last = (ends[-1] + rows - 1) // rows
    lax.fori_loop(0, full, block(False), 0)
    lax.fori_loop(full, last, block(True), 0)
    attended = []
    for h in range(heads):
        acc = acc_ref[h]
        attended.append((acc[:, :LANES] / acc[:, LANES : LANES + 1]).astype(BF16))
    mixed = hidden_ref[...].astype(F32) + dot(jnp.concatenate(attended, axis=1), proj_ref[...])
    chunks = hidden_ref.shape[1] // LANES
    slots = send_ref.shape[0] // chunks
    wide = dot(placed(slot_ref[...], top, slots), mixed.astype(BF16)).astype(BF16)

    def store(first, part):
        send_ref[first : first + part.shape[0], :] = part

    fold_rows(wide, fold_matrix(BLOCK, chunks), store)


def expert_kernel(
    row_ref, cot_ref, weight_ref, out_ref, x_ref, c_ref, grad_ref, *, shards, ff, capacity
):
    slots, width = x_ref.shape
    chunks = width // LANES
    matrix = unfold_matrix(BLOCK, chunks)
    unfold_rows(lambda f, n: row_ref[f : f + n, :], slots, chunks, matrix, x_ref)
    unfold_rows(lambda f, n: cot_ref[f : f + n, :], slots, chunks, matrix, c_ref)
    x, c = x_ref[...], c_ref[...]
    pitch = weight_ref.shape[0] // shards
    step = 256
    gate_sum = jnp.zeros((slots, 1), F32)

    def columns(base, j):
        return jnp.concatenate(
            [
                jnp.concatenate(
                    [
                        weight_ref[
                            s * pitch + base + (j * 2 + i) * LANES : s * pitch
                            + base
                            + (j * 2 + i + 1) * LANES,
                            :,
                        ]
                        for i in range(2)
                    ],
                    axis=1,
                )
                for s in range(shards)
            ],
            axis=0,
        )

    for j in range(ff // step):
        w_gate, w_up = columns(0, j), columns(ff, j)
        w_down = jnp.concatenate(
            [
                weight_ref[s * pitch + 2 * ff + j * step : s * pitch + 2 * ff + (j + 1) * step, :]
                for s in range(shards)
            ],
            axis=1,
        )
        gate_lin = dot(x, w_gate)
        up_lin = dot(x, w_up)
        back = dot(c, w_down, ((1,), (1,)))
        sig = 1.0 / (1.0 + jnp.exp(-gate_lin))
        swish = gate_lin * sig
        up_back = back * swish
        gate_sum = gate_sum + jnp.sum(up_back * up_lin, axis=1, keepdims=True)
        gate_back = back * up_lin * sig * (1.0 + gate_lin * (1.0 - sig))
        part = dot(gate_back.astype(BF16), w_gate, ((1,), (1,))) + dot(
            up_back.astype(BF16), w_up, ((1,), (1,))
        )
        if j == 0:
            grad_ref[...] = part
        else:
            grad_ref[...] += part
    experts = slots // capacity
    each = capacity * chunks

    def store(first, rows):
        size = rows.shape[0]
        at = first
        while at < first + size:
            e, r = at // each, at % each
            n = min(each - r, first + size - at)
            out_ref[e, r : r + n, :] = rows[at - first : at - first + n, :]
            at += n

    fold_rows(grad_ref[...].astype(BF16), fold_matrix(BLOCK, chunks), store)
    high = gate_sum.astype(BF16)
    low = (gate_sum - high.astype(F32)).astype(BF16)
    slot, lane = iota((slots, LANES), 0), iota((slots, LANES), 1)
    rank = slot % capacity
    spread = jnp.where(rank == lane, high.astype(F32), 0.0) + jnp.where(
        rank + 16 == lane, low.astype(F32), 0.0
    )
    owner = as_bf16(iota((experts, slots), 0) == iota((experts, slots), 1) // capacity)
    lines = dot(owner, spread.astype(BF16)).astype(BF16)
    for e in range(experts):
        out_ref[e, each:, :] = jnp.broadcast_to(
            lines[e : e + 1, :], (out_ref.shape[1] - each, LANES)
        )


def combine_kernel(
    back_ref, line_ref, ids_ref, gate_ref, slot_ref, grad_ref, gates_ref, wide_ref, *, capacity
):
    top, tokens = ids_ref.shape
    slots, width = wide_ref.shape
    chunks = width // LANES
    experts = slots // capacity
    each = capacity * chunks

    def load(first, count):
        parts, at = [], first
        while at < first + count:
            e, r = at // each, at % each
            n = min(each - r, first + count - at)
            parts.append(back_ref[e, r : r + n, :])
            at += n
        return jnp.concatenate(parts, axis=0)

    unfold_rows(load, slots, chunks, unfold_matrix(BLOCK, chunks), wide_ref)
    both = slot_ref[...]
    spread = placed(both, top, slots)
    grad_ref[...] = dot(spread, wide_ref[...], ((0,), (0,)))
    lines = line_ref[...]
    expert = iota((experts, tokens), 0)
    rank = iota((LANES, tokens), 0)
    out = []
    for k in range(top):
        own = as_bf16(expert == ids_ref[k : k + 1, :])
        found = dot(lines, own, ((0,), (0,)))
        mine = both[top + k : top + k + 1, :]
        take = jnp.logical_or(rank == mine, rank == mine + 16)
        value = jnp.sum(jnp.where(take, found, 0.0), axis=0, keepdims=True)
        out.append(value / gate_ref[k : k + 1, :].astype(F32))
    gates_ref[...] = jnp.concatenate(out, axis=0).astype(BF16)


def exchange(rows):
    return lax.all_to_all(rows, "exp", split_axis=0, concat_axis=0, tiled=True)


def local(
    hidden,
    queries,
    thinker_keys,
    thinker_values,
    thinker_lengths,
    out_proj,
    expert_ids,
    gate_values,
    w_gate,
    w_up,
    w_down,
    cotangent,
):
    tokens, width = hidden.shape
    top = expert_ids.shape[1]
    experts, shards = lax.axis_size("exp"), lax.axis_size("seq")
    capacity = tokens * top * 5 // (4 * experts)
    slots = experts * capacity
    chunks = width // LANES
    each = capacity * chunks
    ff = w_gate.shape[2]
    own_rows = thinker_keys.shape[0]
    rows = experts * own_rows
    pitch = rows + 16
    place = jnp.stack([lax.axis_index("seq"), lax.axis_index("exp")]).astype(jnp.int32)
    ids, gates = expert_ids.T, gate_values.T

    packed = pl.pallas_call(
        pack_kernel,
        out_shape=jax.ShapeDtypeStruct((experts, own_rows, 3 * LANES), BF16),
        in_specs=[SMEM] + vmem(2),
        out_specs=vmem(1)[0],
        compiler_params=params(16),
        name="pack",
    )(thinker_lengths, thinker_keys, thinker_values)
    kv_rows = exchange(packed)

    slot_table, send_cot = pl.pallas_call(
        functools.partial(dispatch_kernel, experts=experts, capacity=capacity),
        out_shape=(
            jax.ShapeDtypeStruct((2 * top, tokens), jnp.int32),
            jax.ShapeDtypeStruct((slots * chunks, LANES), BF16),
        ),
        in_specs=vmem(3),
        out_specs=tuple(vmem(2)),
        compiler_params=params(24),
        name="dispatch",
    )(ids, gates, cotangent)

    segment = pl.pallas_call(
        functools.partial(segment_kernel, rows=own_rows),
        out_shape=jax.ShapeDtypeStruct((pitch, 2 * LANES), BF16),
        in_specs=vmem(1),
        out_specs=vmem(1)[0],
        compiler_params=params(16),
        name="segment",
    )(kv_rows.reshape(rows, 3 * LANES))
    segment, send_cot = lax.optimization_barrier((segment, send_cot))
    kv_all = lax.all_gather(segment, "seq", axis=0, tiled=True)
    recv_cot = exchange(send_cot.reshape(experts, each, LANES))

    def blocks(w):
        return w[0].reshape(LANES, ff // LANES, LANES).transpose(1, 0, 2).reshape(ff, LANES)

    shard = jnp.concatenate([blocks(w_gate), blocks(w_up), w_down[0]], axis=0)
    kv_all, shard = lax.optimization_barrier((kv_all, shard))
    weights = lax.all_gather(shard, "seq", axis=0, tiled=True)

    send_rows = pl.pallas_call(
        functools.partial(attend_kernel, segments=shards, rows=rows, pitch=pitch, top=top),
        out_shape=jax.ShapeDtypeStruct((slots * chunks, LANES), BF16),
        in_specs=[SMEM, SMEM] + vmem(5),
        out_specs=vmem(1)[0],
        scratch_shapes=[
            pltpu.VMEM((width // LANES, tokens, 1), F32),
            pltpu.VMEM((width // LANES, tokens, 2 * LANES), F32),
        ],
        compiler_params=params(32),
        name="attend",
    )(place, thinker_lengths, kv_all, queries, hidden, out_proj, slot_table)
    send_rows, recv_cot = lax.optimization_barrier((send_rows, recv_cot))
    recv_rows = exchange(send_rows.reshape(experts, each, LANES))

    back = pl.pallas_call(
        functools.partial(expert_kernel, shards=shards, ff=ff, capacity=capacity),
        out_shape=jax.ShapeDtypeStruct((experts, each + 8, LANES), BF16),
        in_specs=vmem(3),
        out_specs=vmem(1)[0],
        scratch_shapes=[
            pltpu.VMEM((slots, width), BF16),
            pltpu.VMEM((slots, width), BF16),
            pltpu.VMEM((slots, width), F32),
        ],
        compiler_params=params(48),
        name="expert",
    )(recv_rows.reshape(slots * chunks, LANES), recv_cot.reshape(slots * chunks, LANES), weights)
    home = exchange(back)

    grad_input, grad_gates = pl.pallas_call(
        functools.partial(combine_kernel, capacity=capacity),
        out_shape=(
            jax.ShapeDtypeStruct((tokens, width), F32),
            jax.ShapeDtypeStruct((top, tokens), BF16),
        ),
        in_specs=vmem(5),
        out_specs=tuple(vmem(2)),
        scratch_shapes=[pltpu.VMEM((slots, width), BF16)],
        compiler_params=params(24),
        name="combine",
    )(home, home[:, each, :], ids, gates, slot_table)
    return grad_input, grad_gates.T


def solution(mesh):
    both = P(("seq", "exp"), None)
    return jax.shard_map(
        local,
        mesh=mesh,
        in_specs=(
            both,
            both,
            both,
            both,
            P(("seq", "exp")),
            P(),
            both,
            both,
            P("exp", "seq", None),
            P("exp", "seq", None),
            P("exp", None, "seq"),
            both,
        ),
        out_specs=(both, both),
        check_vma=False,
    )
```

time: 1150 us -> 226 us (0.20)
  the two profiles are of different devices: /device:TPU:31 before, /device:TPU:16 now
where the time goes in v1:
time: 226 us; the launch traced here: 225 us
  blocking collectives  86.7 us (38%)
  waiting for transfers between devices  64.2 us (28%)
  starting transfers between devices  30.2 us (13%)
  Pallas kernels  19.9 us (9%)
  between operations  14.2 us (6%)
  local copies, waits for them, and re-layouts  8.73 us (4%)
    all_to_all x2, blocking collectives, exchange(): return lax.all_to_all(rows, 'exp', split_axis=0, concat_axis=0, tiled=True)  86.7 us
    all_to_all x2, waiting for transfers between devices, exchange(): return lax.all_to_all(rows, 'exp', split_axis=0, concat_axis=0, tiled=True)  42 us
    all_to_all x2, starting transfers between devices, exchange(): return lax.all_to_all(rows, 'exp', split_axis=0, concat_axis=0, tiled=True)  30.1 us
    all_gather x1, waiting for transfers between devices, local(): kv_all = lax.all_gather(segment, 'seq', axis=0, tiled=True)  22.2 us
    pallas_call x1, Pallas kernels, local(): pl.pallas_call(functools.partial(expert_kernel, shards=shards, ff=ff, cap...  10.2 us
    unnamed x37, local copies, waits for them, and re-layouts  8.36 us
  transfers between devices with their start and end apart: 4, of which 3 were waited for; matrix products, arithmetic and copies ran while one was open for 1% of the time, Pallas kernels for 3%

profile of v1, /device:TPU:16, one launch (start us, length us, event | category | flops | bytes accessed | tf_op | source)
XLA Modules:
  0.0 224.9 jit_solution(10927239070159840924)
XLA Ops:
  7.2 0.7 copy-done.10
  7.9 0.7 copy-done.11
  8.6 0.7 copy-done.12
  9.2 1.3 pack.1
  10.6 16.6 %all-to-all-start = ((bf16[64,8,384]{2,1,0:T(8,128)(2,1)}), bf16[64,8,384]{2,1,0:T(8,128)(2,1)S(1)}, u32[]{:S(2)}, u32[]{:S(2)}) async-start(bf16[64,8,384]{2,1,0:T(8,128)(2,1)} %pack.1), calls=%async_computation | async-start | bytes 786432 | tf_op jit(solution)/shard_map/all_to_all | solution.py:349
  27.2 0.0 all-gather.3.cloned.1.call-start
  27.2 0.7 copy-done.6
  27.9 0.7 copy-done.8
  28.6 2.1 dispatch.1
  30.7 13.1 %all-to-all-done = bf16[64,8,384]{2,1,0:T(8,128)(2,1)S(1)} async-done(((bf16[64,8,384]{2,1,0:T(8,128)(2,1)}), bf16[64,8,384]{2,1,0:T(8,128)(2,1)S(1)}, u32[]{:S(2)}, u32[]{:S(2)}) %all-to-all-start) | async-done | bytes 393248 | tf_op jit(solution)/shard_map/all_to_all | solution.py:349
  43.8 0.8 segment.1
  44.6 0.0 all-gather.3.cloned.1.call-update
  44.7 0.0 all-gather.5.cloned.1.call-start
  44.7 0.2 copy.24
  44.9 0.2 copy.25
  45.1 0.2 copy.26
  45.2 0.2 copy.27
  45.4 0.9 pad_maximum_fusion
  46.3 22.2 %all-gather.3.cloned.1.call-done.kv_ref = bf16[4224,256]{1,0:T(8,128)(2,1)} async-done(((bf16[528,256]{1,0:T(8,128)(2,1)}), bf16[4224,256]{1,0:T(8,128)(2,1)}) %all-gather.3.cloned.1.call-update) | async-done | bytes 2162704 | tf_op jit(solution)/shard_map/all_gather | solution.py:411
  68.6 0.0 all-gather.5.cloned.1.call-update
  68.6 0.0 copy-start.3
  68.6 13.5 %all-to-all-start.1 = ((bf16[64,80,128]{2,1,0:T(8,128)(2,1)}), bf16[64,80,128]{2,1,0:T(8,128)(2,1)S(1)}, u32[]{:S(2)}, u32[]{:S(2)}) async-start(bf16[64,80,128]{2,1,0:T(8,128)(2,1)} %bitcast.12), calls=%async_computation.1 | async-start | bytes 2621440 | tf_op jit(solution)/shard_map/all_to_all | solution.py:349
  82.1 0.1 pad_add_fusion.place_ref
  82.2 1.6 copy-done.1
  83.8 1.7 copy-done.2
  85.5 3.8 %attend.1 = bf16[5120,128]{1,0:T(8,128)(2,1)S(1)} custom-call(s32[2]{0:T(128)S(1)} %pad_add_fusion.place_ref, s32[4]{0:T(128)S(1)} %copy-done.13, bf16[4224,256]{1,0:T(8,128)(2,1)S(1)} %copy-done.1, bf16[128,1024]{1,0:T(8,128)(2,1)S(1)} %copy-done.3, bf16[128,1024]{1,0:T(8,128)(2,1)S(1)} %copy-done.4, bf16[1024,1024]{1,0:T(8,128)(2,1)S(1)} %copy-done.2, ...), custom_call_target="tpu_custom_call" | custom-call | tf_op jit(solution)/shard_map/attend/pallas_call | solution.py:421
  89.3 28.9 %all-to-all-done.1 = bf16[64,80,128]{2,1,0:T(8,128)(2,1)S(1)} async-done(((bf16[64,80,128]{2,1,0:T(8,128)(2,1)}), bf16[64,80,128]{2,1,0:T(8,128)(2,1)S(1)}, u32[]{:S(2)}, u32[]{:S(2)}) %all-to-all-start.1) | async-done | bytes 1310752 | tf_op jit(solution)/shard_map/all_to_all | solution.py:349
  118.2 42.9 %all_to_all.20 = bf16[64,80,128]{2,1,0:T(8,128)(2,1)} all-to-all(bf16[64,80,128]{2,1,0:T(8,128)(2,1)S(1)} %bitcast.22), channel_id=1, replica_groups=mesh['seq'=8,'exp'=64] {'exp'}, dimensions={0} | all-to-all | bytes 2621440 | tf_op jit(solution)/shard_map/all_to_all | solution.py:349
  161.1 1.3 copy-done
  162.4 10.2 %expert.1 = bf16[64,88,128]{2,1,0:T(8,128)(2,1)S(1)} custom-call(bf16[5120,128]{1,0:T(8,128)(2,1)S(1)} %bitcast.24, bf16[5120,128]{1,0:T(8,128)(2,1)S(1)} %bitcast.23, bf16[18432,128]{1,0:T(8,128)(2,1)} %all-gather.5.cloned.1.call-done.weight_ref), custom_call_target="tpu_custom_call" | custom-call | tf_op jit(solution)/shard_map/expert/pallas_call | solution.py:436
  172.6 43.8 %all_to_all.21.back_ref = bf16[64,88,128]{2,1,0:T(8,128)(2,1)S(1)} all-to-all(bf16[64,88,128]{2,1,0:T(8,128)(2,1)S(1)} %expert.1), channel_id=1, replica_groups=mesh['seq'=8,'exp'=64] {'exp'}, dimensions={0} | all-to-all | bytes 2883584 | tf_op jit(solution)/shard_map/all_to_all | solution.py:349
  216.4 1.7 combine.1
  (28 shorter events, 0.1 us)
Async XLA Ops:
  7.2 20.1 %copy-start.5 = (bf16[128,1024]{1,0:T(8,128)(2,1)S(1)}, bf16[128,1024]{1,0:T(8,128)(2,1)}, u32[]{:S(2)}) copy-start(bf16[128,1024]{1,0:T(8,128)(2,1)} %cot_ref.1) | copy-start | bytes 786436
  7.2 0.7 copy-start.10
  7.9 0.7 copy-start.11
  8.6 0.7 copy-start.12
  9.2 35.5 %copy-start.15 = (bf16[1,128,768]{2,1,0:T(8,128)(2,1)S(1)}, bf16[1,128,768]{2,1,0:T(8,128)(2,1)}, u32[]{:S(2)}) copy-start(bf16[1,128,768]{2,1,0:T(8,128)(2,1)} %param.20) | copy-start | bytes 589828
  10.6 34.5 %copy-start.16 = (bf16[1,128,768]{2,1,0:T(8,128)(2,1)S(1)}, bf16[1,128,768]{2,1,0:T(8,128)(2,1)}, u32[]{:S(2)}) copy-start(bf16[1,128,768]{2,1,0:T(8,128)(2,1)} %param.21) | copy-start | bytes 589828
  10.6 33.3 %all-to-all-start = ((bf16[64,8,384]{2,1,0:T(8,128)(2,1)}), bf16[64,8,384]{2,1,0:T(8,128)(2,1)S(1)}, u32[]{:S(2)}, u32[]{:S(2)}) async-start(bf16[64,8,384]{2,1,0:T(8,128)(2,1)} %pack.1), calls=%async_computation | async-start | bytes 786432 | tf_op jit(solution)/shard_map/all_to_all | solution.py:349
  27.2 41.4 %all-gather.3.cloned.1.call-start = ((), (), s32[]{:S(2)}) async-start(), calls=%async_computation.4 | async-start | bytes 2433024 | tf_op jit(solution)/shard_map/all_gather | solution.py:411
  27.2 0.7 copy-start.6
  27.9 0.7 copy-start.8
  30.7 14.7 %copy-start.14 = (bf16[1,768,128]{2,1,0:T(8,128)(2,1)S(1)}, bf16[1,768,128]{2,1,0:T(8,128)(2,1)}, u32[]{:S(2)}) copy-start(bf16[1,768,128]{2,1,0:T(8,128)(2,1)} %param.22) | copy-start | bytes 589828
  44.7 116.4 %all-gather.5.cloned.1.call-start = ((), (), s32[]{:S(2)}) async-start(), calls=%async_computation.5 | async-start | bytes 5308416 | tf_op jit(solution)/shard_map/all_gather | solution.py:419
  68.6 13.6 %copy-start.3 = (bf16[128,1024]{1,0:T(8,128)(2,1)S(1)}, bf16[128,1024]{1,0:T(8,128)(2,1)}, u32[]{:S(2)}) copy-start(bf16[128,1024]{1,0:T(8,128)(2,1)} %query_ref.1) | copy-start | bytes 786436
  68.6 13.6 %copy-start.4 = (bf16[128,1024]{1,0:T(8,128)(2,1)S(1)}, bf16[128,1024]{1,0:T(8,128)(2,1)}, u32[]{:S(2)}) copy-start(bf16[128,1024]{1,0:T(8,128)(2,1)} %hidden_ref.1) | copy-start | bytes 786436
  68.6 13.6 %copy-start.13 = (s32[4]{0:T(128)S(1)}, s32[4]{0:T(128)}, u32[]{:S(2)}) copy-start(s32[4]{0:T(128)} %lens_ref.3) | copy-start | bytes 52
  68.6 49.6 %all-to-all-start.1 = ((bf16[64,80,128]{2,1,0:T(8,128)(2,1)}), bf16[64,80,128]{2,1,0:T(8,128)(2,1)S(1)}, u32[]{:S(2)}, u32[]{:S(2)}) async-start(bf16[64,80,128]{2,1,0:T(8,128)(2,1)} %bitcast.12), calls=%async_computation.1 | async-start | bytes 2621440 | tf_op jit(solution)/shard_map/all_to_all | solution.py:349
  82.2 1.6 copy-start.1
  83.8 1.7 copy-start.2
  161.1 1.3 copy-start
  172.6 43.9 %copy-start.7 = (s32[128,4]{0,1:T(4,128)S(1)}, s32[128,4]{0,1:T(4,128)}, u32[]{:S(2)}) copy-start(s32[128,4]{0,1:T(4,128)} %param.18) | copy-start | bytes 6148
  172.6 43.9 %copy-start.9 = (bf16[128,4]{0,1:T(4,128)(2,1)S(1)}, bf16[128,4]{0,1:T(4,128)(2,1)}, u32[]{:S(2)}) copy-start(bf16[128,4]{0,1:T(4,128)(2,1)} %param.19) | copy-start | bytes 3076
Sparse Core Ops, SparseCore 0:
  44.8 23.7 all-gather.2
  70.7 40.0 all-gather.4

commit v2 on v1

--- a/solution.py
+++ b/solution.py
@@ -154,19 +154,36 @@
     send_ref,
     max_ref,
     acc_ref,
+    kv_buf,
+    proj_buf,
+    kv_sem,
+    proj_sem,
     *,
     segments,
     rows,
     pitch,
     top,
+    together,
 ):
+    def kv_copy(b):
+        return pltpu.make_async_copy(kv_ref.at[b], kv_buf.at[b], kv_sem.at[b])
+
+    proj_copy = pltpu.make_async_copy(proj_ref, proj_buf, proj_sem)
+    for b in range(segments):
+        kv_copy(b).start()
+    proj_copy.start()
     tokens = query_ref.shape[0]
     heads = query_ref.shape[1] // LANES
+    scale = LANES**-0.5 * 1.4426950408889634
+    max_ref[...] = jnp.full(max_ref.shape, NEG, F32)
+    acc_ref[...] = jnp.zeros(acc_ref.shape, F32)
+    for b in range(segments):
+        kv_copy(b).wait()
     seq, exp = place_ref[0], place_ref[1]
     total = jnp.zeros((16, LANES), F32)
     lane = iota((16, LANES), 1)
     for s in range(segments):
-        line = kv_ref[s * pitch + rows : s * pitch + rows + 16, 0:LANES].astype(F32)
+        line = kv_buf[s, rows : rows + 16, 0:LANES].astype(F32)
         take = jnp.logical_or(seq > s, jnp.logical_and(seq == s, lane < exp))
         total = total + jnp.where(take, line, 0.0)
     offset = (jnp.sum(total) * (1.0 / 16.0)).astype(jnp.int32)
@@ -174,33 +191,32 @@
     for g in range(lens_ref.shape[0]):
         offset = offset + lens_ref[g]
         ends.append(offset)
-    group = iota((tokens, 1), 0) // GROUP
-    limits = jnp.zeros((tokens, 1), jnp.int32)
+    size = together * tokens
+    group = (iota((size, 1), 0) % tokens) // GROUP
+    limits = jnp.zeros((size, 1), jnp.int32)
     for g, end in enumerate(ends):
         limits = jnp.where(group == g, end, limits)
-    scale = LANES**-0.5 * 1.4426950408889634
-    max_ref[...] = jnp.full(max_ref.shape, NEG, F32)
-    acc_ref[...] = jnp.zeros(acc_ref.shape, F32)
     ones = as_bf16(iota((rows, LANES), 1) == 0)
 
     def block(masked):
         def body(b, carry):
-            first = pl.multiple_of(b * pitch, 16)
-            keys = kv_ref[pl.ds(first, rows), 0:LANES]
-            values = kv_ref[pl.ds(first, rows), LANES : 2 * LANES]
-            wide = jnp.concatenate([values, ones], axis=1)
-            for h in range(heads):
-                q = query_ref[:, h * LANES : (h + 1) * LANES]
+            keys = kv_buf[b, 0:rows, 0:LANES]
+            wide = jnp.concatenate([kv_buf[b, 0:rows, LANES : 2 * LANES], ones], axis=1)
+            for h in range(0, heads, together):
+                q = jnp.concatenate(
+                    [query_ref[:, i * LANES : (i + 1) * LANES] for i in range(h, h + together)],
+                    axis=0,
+                )
+                at = slice(h * tokens, h * tokens + size)
                 s = dot(q, keys, ((1,), (1,)))
                 if masked:
-                    seen = iota((tokens, rows), 1) + b * rows < limits
-                    s = jnp.where(seen, s, NEG)
-                old = max_ref[h]
+                    s = jnp.where(iota((size, rows), 1) + b * rows < limits, s, NEG)
+                old = max_ref[at, :]
                 new = jnp.maximum(old, jnp.max(s, axis=1, keepdims=True))
-                max_ref[h] = new
+                max_ref[at, :] = new
                 w = jnp.exp2((s - new) * scale).astype(BF16)
                 factor = jnp.exp2((old - new) * scale)
-                acc_ref[h] = acc_ref[h] * factor + dot(w, wide)
+                acc_ref[at, :] = acc_ref[at, :] * factor + dot(w, wide)
             return carry
 
         return body
@@ -211,9 +227,10 @@
     lax.fori_loop(full, last, block(True), 0)
     attended = []
     for h in range(heads):
-        acc = acc_ref[h]
+        acc = acc_ref[h * tokens : (h + 1) * tokens, :]
         attended.append((acc[:, :LANES] / acc[:, LANES : LANES + 1]).astype(BF16))
-    mixed = hidden_ref[...].astype(F32) + dot(jnp.concatenate(attended, axis=1), proj_ref[...])
+    proj_copy.wait()
+    mixed = hidden_ref[...].astype(F32) + dot(jnp.concatenate(attended, axis=1), proj_buf[...])
     chunks = hidden_ref.shape[1] // LANES
     slots = send_ref.shape[0] // chunks
     wide = dot(placed(slot_ref[...], top, slots), mixed.astype(BF16)).astype(BF16)
@@ -224,41 +241,23 @@
     fold_rows(wide, fold_matrix(BLOCK, chunks), store)
 
 
-def expert_kernel(
-    row_ref, cot_ref, weight_ref, out_ref, x_ref, c_ref, grad_ref, *, shards, ff, capacity
-):
-    slots, width = x_ref.shape
+def prepare_kernel(cot_ref, weight_ref, gate_ref, up_ref, back_ref, c_ref, *, shards, ff):
+    slots, width = c_ref.shape
     chunks = width // LANES
-    matrix = unfold_matrix(BLOCK, chunks)
-    unfold_rows(lambda f, n: row_ref[f : f + n, :], slots, chunks, matrix, x_ref)
-    unfold_rows(lambda f, n: cot_ref[f : f + n, :], slots, chunks, matrix, c_ref)
-    x, c = x_ref[...], c_ref[...]
     pitch = weight_ref.shape[0] // shards
+    for s in range(shards):
+        for i in range(ff // LANES):
+            for base, ref in ((0, gate_ref), (ff, up_ref)):
+                at = s * pitch + base + i * LANES
+                ref[s * LANES : (s + 1) * LANES, i * LANES : (i + 1) * LANES] = weight_ref[
+                    at : at + LANES, :
+                ]
+    unfold_rows(
+        lambda f, n: cot_ref[f : f + n, :], slots, chunks, unfold_matrix(BLOCK, chunks), c_ref
+    )
+    c = c_ref[...]
     step = 256
-    gate_sum = jnp.zeros((slots, 1), F32)
-
-    def columns(base, j):
-        return jnp.concatenate(
-            [
-                jnp.concatenate(
-                    [
-                        weight_ref[
-                            s * pitch + base + (j * 2 + i) * LANES : s * pitch
-                            + base
-                            + (j * 2 + i + 1) * LANES,
-                            :,
-                        ]
-                        for i in range(2)
-                    ],
-                    axis=1,
-                )
-                for s in range(shards)
-            ],
-            axis=0,
-        )
-
     for j in range(ff // step):
-        w_gate, w_up = columns(0, j), columns(ff, j)
         w_down = jnp.concatenate(
             [
                 weight_ref[s * pitch + 2 * ff + j * step : s * pitch + 2 * ff + (j + 1) * step, :]
@@ -266,14 +265,54 @@
             ],
             axis=1,
         )
+        back_ref[:, j * step : (j + 1) * step] = dot(c, w_down, ((1,), (1,)))
+
+
+def expert_kernel(
+    row_ref,
+    gate_ref,
+    up_ref,
+    back_ref,
+    out_ref,
+    x_ref,
+    grad_ref,
+    gate_buf,
+    up_buf,
+    back_buf,
+    other_sem,
+    *,
+    capacity,
+):
+    slots, width = x_ref.shape
+    chunks = width // LANES
+    ff = gate_ref.shape[1]
+    others = [
+        pltpu.make_async_copy(src, dst, other_sem.at[i])
+        for i, (src, dst) in enumerate(
+            ((gate_ref, gate_buf), (up_ref, up_buf), (back_ref, back_buf))
+        )
+    ]
+    for copy in others:
+        copy.start()
+    unfold_rows(
+        lambda f, n: row_ref[f : f + n, :], slots, chunks, unfold_matrix(BLOCK, chunks), x_ref
+    )
+    x = x_ref[...]
+    for copy in others:
+        copy.wait()
+    step = 256
+    gate_sum = jnp.zeros((slots, 1), F32)
+    for j in range(ff // step):
+        at = slice(j * step, (j + 1) * step)
+        w_gate, w_up = gate_buf[:, at], up_buf[:, at]
+        back = back_buf[:, at]
         gate_lin = dot(x, w_gate)
         up_lin = dot(x, w_up)
-        back = dot(c, w_down, ((1,), (1,)))
-        sig = 1.0 / (1.0 + jnp.exp(-gate_lin))
+        sig = 0.5 * jnp.tanh(0.5 * gate_lin) + 0.5
         swish = gate_lin * sig
         up_back = back * swish
         gate_sum = gate_sum + jnp.sum(up_back * up_lin, axis=1, keepdims=True)
-        gate_back = back * up_lin * sig * (1.0 + gate_lin * (1.0 - sig))
+        gate_back = back * up_lin * (sig + swish * (1.0 - sig))
         part = dot(gate_back.astype(BF16), w_gate, ((1,), (1,))) + dot(
             up_back.astype(BF16), w_up, ((1,), (1,))
         )
@@ -343,6 +382,57 @@
         value = jnp.sum(jnp.where(take, found, 0.0), axis=0, keepdims=True)
         out.append(value / gate_ref[k : k + 1, :].astype(F32))
     gates_ref[...] = jnp.concatenate(out, axis=0).astype(BF16)
+
+
+HBM = pl.BlockSpec(memory_space=pltpu.HBM)
+TOGETHER = 2
+
+
+def attend(place, lens, kv, queries, hidden, proj, slot_table, *, rows, slots):
+    tokens, width = hidden.shape
+    segments, pitch = kv.shape[0], kv.shape[1]
+    top = slot_table.shape[0] // 2
+    heads, chunks = queries.shape[1] // LANES, width // LANES
+    return pl.pallas_call(
+        functools.partial(
+            attend_kernel, segments=segments, rows=rows, pitch=pitch, top=top, together=TOGETHER
+        ),
+        out_shape=jax.ShapeDtypeStruct((slots * chunks, LANES), BF16),
+        in_specs=[SMEM, SMEM, HBM] + vmem(2) + [HBM] + vmem(1),
+        out_specs=vmem(1)[0],
+        scratch_shapes=[
+            pltpu.VMEM((heads * tokens, 1), F32),
+            pltpu.VMEM((heads * tokens, 2 * LANES), F32),
+            pltpu.VMEM(kv.shape, BF16),
+            pltpu.VMEM(proj.shape, BF16),
+            pltpu.SemaphoreType.DMA((segments,)),
+            pltpu.SemaphoreType.DMA(()),
+        ],
+        compiler_params=params(58),
+        cost_estimate=pl.CostEstimate(flops=0, bytes_accessed=0, transcendentals=0),
+        name="attend",
+    )(place, lens, kv, queries, hidden, proj, slot_table)
+
+
+def expert(rows, gate, up, back, *, capacity):
+    slots, (width, ff) = back.shape[0], gate.shape
+    chunks = width // LANES
+    return pl.pallas_call(
+        functools.partial(expert_kernel, capacity=capacity),
+        out_shape=jax.ShapeDtypeStruct((slots // capacity, capacity * chunks + 8, LANES), BF16),
+        in_specs=vmem(1) + [HBM] * 3,
+        out_specs=vmem(1)[0],
+        scratch_shapes=[
+            pltpu.VMEM((slots, width), BF16),
+            pltpu.VMEM((slots, width), F32),
+            pltpu.VMEM(gate.shape, BF16),
+            pltpu.VMEM(up.shape, BF16),
+            pltpu.VMEM(back.shape, F32),
+            pltpu.SemaphoreType.DMA((3,)),
+        ],
+        compiler_params=params(50),
+        name="expert",
+    )(rows, gate, up, back)
 
 
 def exchange(rows):
@@ -407,45 +497,48 @@
         compiler_params=params(16),
         name="segment",
     )(kv_rows.reshape(rows, 3 * LANES))
-    segment, send_cot = lax.optimization_barrier((segment, send_cot))
+    def blocks(w):
+        return w[0].reshape(LANES, ff // LANES, LANES).transpose(1, 0, 2).reshape(ff, LANES)
+
+    shard = jnp.concatenate([blocks(w_gate), blocks(w_up), w_down[0]], axis=0)
+    segment, send_cot, shard = lax.optimization_barrier((segment, send_cot, shard))
     kv_all = lax.all_gather(segment, "seq", axis=0, tiled=True)
     recv_cot = exchange(send_cot.reshape(experts, each, LANES))
-
-    def blocks(w):
-        return w[0].reshape(LANES, ff // LANES, LANES).transpose(1, 0, 2).reshape(ff, LANES)
-
-    shard = jnp.concatenate([blocks(w_gate), blocks(w_up), w_down[0]], axis=0)
-    kv_all, shard = lax.optimization_barrier((kv_all, shard))
     weights = lax.all_gather(shard, "seq", axis=0, tiled=True)
 
-    send_rows = pl.pallas_call(
-        functools.partial(attend_kernel, segments=shards, rows=rows, pitch=pitch, top=top),
-        out_shape=jax.ShapeDtypeStruct((slots * chunks, LANES), BF16),
-        in_specs=[SMEM, SMEM] + vmem(5),
-        out_specs=vmem(1)[0],
-        scratch_shapes=[
-            pltpu.VMEM((width // LANES, tokens, 1), F32),
-            pltpu.VMEM((width // LANES, tokens, 2 * LANES), F32),
-        ],
-        compiler_params=params(32),
-        name="attend",
-    )(place, thinker_lengths, kv_all, queries, hidden, out_proj, slot_table)
+    send_rows = attend(
+        place,
+        thinker_lengths,
+        kv_all.reshape(shards, pitch, 2 * LANES),
+        queries,
+        hidden,
+        out_proj,
+        slot_table,
+        rows=rows,
+        slots=slots,
+    )
     send_rows, recv_cot = lax.optimization_barrier((send_rows, recv_cot))
     recv_rows = exchange(send_rows.reshape(experts, each, LANES))
-
-    back = pl.pallas_call(
-        functools.partial(expert_kernel, shards=shards, ff=ff, capacity=capacity),
-        out_shape=jax.ShapeDtypeStruct((experts, each + 8, LANES), BF16),
-        in_specs=vmem(3),
-        out_specs=vmem(1)[0],
-        scratch_shapes=[
-            pltpu.VMEM((slots, width), BF16),
-            pltpu.VMEM((slots, width), BF16),
-            pltpu.VMEM((slots, width), F32),
-        ],
-        compiler_params=params(48),
-        name="expert",
-    )(recv_rows.reshape(slots * chunks, LANES), recv_cot.reshape(slots * chunks, LANES), weights)
+    full_gate, full_up, down_back = pl.pallas_call(
+        functools.partial(prepare_kernel, shards=shards, ff=ff),
+        out_shape=(
+            jax.ShapeDtypeStruct((width, ff), BF16),
+            jax.ShapeDtypeStruct((width, ff), BF16),
+            jax.ShapeDtypeStruct((slots, ff), F32),
+        ),
+        in_specs=vmem(2),
+        out_specs=tuple(vmem(3)),
+        scratch_shapes=[pltpu.VMEM((slots, width), BF16)],
+        compiler_params=params(24),
+        cost_estimate=pl.CostEstimate(
+            flops=40 * slots * width * ff, bytes_accessed=0, transcendentals=0
+        ),
+        name="prepare",
+    )(recv_cot.reshape(slots * chunks, LANES), weights)
+
+    back = expert(
+        recv_rows.reshape(slots * chunks, LANES), full_gate, full_up, down_back, capacity=capacity
+    )
     home = exchange(back)
 
     grad_input, grad_gates = pl.pallas_call(

time: 226 us -> 197 us (0.87)
  the two profiles are of different devices: /device:TPU:16 before, /device:TPU:22 now
where the time goes in v2:
time: 197 us
  waiting for transfers between devices  60.5 us (31%)
  blocking collectives  48.9 us (25%)
  starting transfers between devices  31.5 us (16%)
  Pallas kernels  30.9 us (16%)
  between operations  14.2 us (7%)
  local copies, waits for them, and re-layouts  9.28 us (5%)
    all_to_all x1, blocking collectives, exchange(): return lax.all_to_all(rows, 'exp', split_axis=0, concat_axis=0, tiled=True)  48.9 us
    all_to_all x3, starting transfers between devices, exchange(): return lax.all_to_all(rows, 'exp', split_axis=0, concat_axis=0, tiled=True)  31.4 us
    all_to_all x3, waiting for transfers between devices, exchange(): return lax.all_to_all(rows, 'exp', split_axis=0, concat_axis=0, tiled=True)  30.3 us
    all_gather x1, waiting for transfers between devices, local(): kv_all = lax.all_gather(segment, 'seq', axis=0, tiled=True)  16.1 us
    pallas_call x1, Pallas kernels, attend(): pl.pallas_call(functools.partial(attend_kernel, segments=segments, rows=r...  14.8 us
    all_gather x1, waiting for transfers between devices, local(): weights = lax.all_gather(shard, 'seq', axis=0, tiled=True)  13.4 us
    unnamed x33, local copies, waits for them, and re-layouts  8.9 us
    pallas_call x1, Pallas kernels, expert(): pl.pallas_call(functools.partial(expert_kernel, capacity=capacity), out_s...  8.08 us
  transfers between devices with their start and end apart: 5, of which 5 were waited for; matrix products, arithmetic and copies ran while one was open for 1% of the time, Pallas kernels for 10%

profile of v2, /device:TPU:22, one launch (start us, length us, event | category | flops | bytes accessed | tf_op | source)
XLA Modules:
  0.0 196.6 jit_solution(11102131971110019750)
XLA Ops:
  7.2 0.7 copy-done.8
  7.9 0.7 copy-done.9
  8.6 0.7 copy-done.10
  9.3 1.3 pack.1
  10.6 16.6 %all-to-all-start = ((bf16[64,8,384]{2,1,0:T(8,128)(2,1)}), bf16[64,8,384]{2,1,0:T(8,128)(2,1)S(1)}, u32[]{:S(2)}, u32[]{:S(2)}) async-start(bf16[64,8,384]{2,1,0:T(8,128)(2,1)} %pack.1), calls=%async_computation | async-start | bytes 786432 | tf_op jit(solution)/shard_map/all_to_all | solution.py:439
  27.2 0.0 all-gather.3.cloned.1.call-start
  27.3 0.2 copy.24
  27.4 0.2 copy.25
  27.6 0.2 copy.26
  27.8 0.2 copy.27
  28.0 2.1 %dispatch.1 = (s32[8,128]{1,0:T(8,128)S(1)}, bf16[5120,128]{1,0:T(8,128)(2,1)}) custom-call(s32[4,128]{1,0:T(4,128)S(1)} %bitcast.27, bf16[4,128]{1,0:T(4,128)(2,1)S(1)} %bitcast.29, bf16[128,1024]{1,0:T(8,128)(2,1)S(1)} %copy-done.3), custom_call_target="tpu_custom_call" | custom-call | tf_op jit(solution)/shard_map/dispatch/pallas_call | solution.py:480
  30.1 0.6 copy-done.4
  30.7 0.8 pad_maximum_fusion
  31.5 12.3 %all-to-all-done = bf16[64,8,384]{2,1,0:T(8,128)(2,1)S(1)} async-done(((bf16[64,8,384]{2,1,0:T(8,128)(2,1)}), bf16[64,8,384]{2,1,0:T(8,128)(2,1)S(1)}, u32[]{:S(2)}, u32[]{:S(2)}) %all-to-all-start) | async-done | bytes 393248 | tf_op jit(solution)/shard_map/all_to_all | solution.py:439
  43.8 0.8 segment.1
  44.7 0.7 all-gather.5.cloned.1.call-update
  45.4 5.2 %all-to-all-start.1 = ((bf16[64,80,128]{2,1,0:T(8,128)(2,1)}), bf16[64,80,128]{2,1,0:T(8,128)(2,1)S(1)}, u32[]{:S(2)}, u32[]{:S(2)}) async-start(bf16[64,80,128]{2,1,0:T(8,128)(2,1)} %bitcast.13), calls=%async_computation.1 | async-start | bytes 2621440 | tf_op jit(solution)/shard_map/all_to_all | solution.py:439
  50.6 0.6 pad_add_fusion.place_ref
  51.2 16.1 %all-gather.3.cloned.1.call-done = bf16[4224,256]{1,0:T(8,128)(2,1)} async-done(((bf16[528,256]{1,0:T(8,128)(2,1)}), bf16[4224,256]{1,0:T(8,128)(2,1)}) %all-gather.3.cloned.1.call-update) | async-done | bytes 2162704 | tf_op jit(solution)/shard_map/all_gather | solution.py:505
  67.3 14.8 %attend.1 = bf16[5120,128]{1,0:T(8,128)(2,1)} custom-call(s32[2]{0:T(128)} %pad_add_fusion.place_ref, s32[4]{0:T(128)} %lens_ref.3, bf16[8,528,256]{2,1,0:T(8,128)(2,1)} %bitcast.32, bf16[128,1024]{1,0:T(8,128)(2,1)} %query_ref.1, bf16[128,1024]{1,0:T(8,128)(2,1)} %hidden_ref.1, bf16[1024,1024]{1,0:T(8,128)(2,1)} %proj_ref.1, s32[8,128]{1,0:T(8,128)} %copy-done.4), custom_call_target="tpu_custom_call" | custom-call | tf_op jit(solution)/shard_map/attend/pallas_call | solution.py:396
  82.1 3.7 %all-to-all-done.1 = bf16[64,80,128]{2,1,0:T(8,128)(2,1)S(1)} async-done(((bf16[64,80,128]{2,1,0:T(8,128)(2,1)}), bf16[64,80,128]{2,1,0:T(8,128)(2,1)S(1)}, u32[]{:S(2)}, u32[]{:S(2)}) %all-to-all-start.1) | async-done | bytes 1310752 | tf_op jit(solution)/shard_map/all_to_all | solution.py:439
  85.8 9.6 %all-to-all-start.2 = ((bf16[64,80,128]{2,1,0:T(8,128)(2,1)}), bf16[64,80,128]{2,1,0:T(8,128)(2,1)S(1)}, u32[]{:S(2)}, u32[]{:S(2)}) async-start(bf16[64,80,128]{2,1,0:T(8,128)(2,1)} %bitcast.31), calls=%async_computation.2 | async-start | bytes 2621440 | tf_op jit(solution)/shard_map/all_to_all | solution.py:439
  95.5 13.4 %all-gather.5.cloned.1.call-done.weight_ref = bf16[18432,128]{1,0:T(8,128)(2,1)} async-done(((bf16[2304,128]{1,0:T(8,128)(2,1)}), bf16[18432,128]{1,0:T(8,128)(2,1)}) %all-gather.5.cloned.1.call-update) | async-done | bytes 4718608 | tf_op jit(solution)/shard_map/all_gather | solution.py:507
  108.9 2.3 %copy-done.11 = bf16[18432,128]{1,0:T(8,128)(2,1)S(1)} copy-done((bf16[18432,128]{1,0:T(8,128)(2,1)S(1)}, bf16[18432,128]{1,0:T(8,128)(2,1)}, u32[]{:S(2)}) %copy-start.11) | copy-done | bytes 4718616
  111.2 2.1 %prepare.1 = (bf16[1024,768]{1,0:T(8,128)(2,1)S(1)}, bf16[1024,768]{1,0:T(8,128)(2,1)S(1)}, f32[640,768]{1,0:T(8,128)S(1)}) custom-call(bf16[5120,128]{1,0:T(8,128)(2,1)S(1)} %bitcast.25, bf16[18432,128]{1,0:T(8,128)(2,1)S(1)} %copy-done.11), custom_call_target="tpu_custom_call" | custom-call | flops 20132659200 | tf_op jit(solution)/shard_map/prepare/pallas_call | solution.py:522
  113.3 1.3 copy-done
  114.5 1.1 copy-done.1
  115.7 1.2 copy-done.2
  116.8 14.2 %all-to-all-done.2 = bf16[64,80,128]{2,1,0:T(8,128)(2,1)S(1)} async-done(((bf16[64,80,128]{2,1,0:T(8,128)(2,1)}), bf16[64,80,128]{2,1,0:T(8,128)(2,1)S(1)}, u32[]{:S(2)}, u32[]{:S(2)}) %all-to-all-start.2) | async-done | bytes 1310752 | tf_op jit(solution)/shard_map/all_to_all | solution.py:439
  131.1 8.1 %expert.1 = bf16[64,88,128]{2,1,0:T(8,128)(2,1)S(1)} custom-call(bf16[5120,128]{1,0:T(8,128)(2,1)S(1)} %bitcast.23, bf16[1024,768]{1,0:T(8,128)(2,1)} %copy-done.1, bf16[1024,768]{1,0:T(8,128)(2,1)} %copy-done.2, f32[640,768]{1,0:T(8,128)} %copy-done), custom_call_target="tpu_custom_call" | custom-call | tf_op jit(solution)/shard_map/expert/pallas_call | solution.py:420
  139.2 48.9 %all_to_all.20.back_ref = bf16[64,88,128]{2,1,0:T(8,128)(2,1)S(1)} all-to-all(bf16[64,88,128]{2,1,0:T(8,128)(2,1)S(1)} %expert.1), channel_id=1, replica_groups=mesh['seq'=8,'exp'=64] {'exp'}, dimensions={0} | all-to-all | bytes 2883584 | tf_op jit(solution)/shard_map/all_to_all | solution.py:439
  188.1 1.7 combine.1
  (26 shorter events, 0.1 us)
Async XLA Ops:
  7.2 20.8 %copy-start.3 = (bf16[128,1024]{1,0:T(8,128)(2,1)S(1)}, bf16[128,1024]{1,0:T(8,128)(2,1)}, u32[]{:S(2)}) copy-start(bf16[128,1024]{1,0:T(8,128)(2,1)} %cot_ref.1) | copy-start | bytes 786436
  7.2 20.8 %copy-start.7 = (bf16[128,4]{0,1:T(4,128)(2,1)S(1)}, bf16[128,4]{0,1:T(4,128)(2,1)}, u32[]{:S(2)}) copy-start(bf16[128,4]{0,1:T(4,128)(2,1)} %param.19) | copy-start | bytes 3076
  7.2 20.8 %copy-start.6 = (s32[128,4]{0,1:T(4,128)S(1)}, s32[128,4]{0,1:T(4,128)}, u32[]{:S(2)}) copy-start(s32[128,4]{0,1:T(4,128)} %param.18) | copy-start | bytes 6148
  7.2 0.7 copy-start.8
  7.9 0.7 copy-start.9
  8.6 0.7 copy-start.10
  9.3 18.0 %copy-start.13 = (bf16[1,128,768]{2,1,0:T(8,128)(2,1)S(1)}, bf16[1,128,768]{2,1,0:T(8,128)(2,1)}, u32[]{:S(2)}) copy-start(bf16[1,128,768]{2,1,0:T(8,128)(2,1)} %param.20) | copy-start | bytes 589828
  9.3 18.3 %copy-start.14 = (bf16[1,128,768]{2,1,0:T(8,128)(2,1)S(1)}, bf16[1,128,768]{2,1,0:T(8,128)(2,1)}, u32[]{:S(2)}) copy-start(bf16[1,128,768]{2,1,0:T(8,128)(2,1)} %param.21) | copy-start | bytes 589828
  10.6 20.1 %copy-start.12 = (bf16[1,768,128]{2,1,0:T(8,128)(2,1)S(1)}, bf16[1,768,128]{2,1,0:T(8,128)(2,1)}, u32[]{:S(2)}) copy-start(bf16[1,768,128]{2,1,0:T(8,128)(2,1)} %param.22) | copy-start | bytes 589828
  10.6 33.3 %all-to-all-start = ((bf16[64,8,384]{2,1,0:T(8,128)(2,1)}), bf16[64,8,384]{2,1,0:T(8,128)(2,1)S(1)}, u32[]{:S(2)}, u32[]{:S(2)}) async-start(bf16[64,8,384]{2,1,0:T(8,128)(2,1)} %pack.1), calls=%async_computation | async-start | bytes 786432 | tf_op jit(solution)/shard_map/all_to_all | solution.py:439
  27.2 40.1 %all-gather.3.cloned.1.call-start = ((), (), s32[]{:S(2)}) async-start(), calls=%async_computation.4 | async-start | bytes 2433024 | tf_op jit(solution)/shard_map/all_gather | solution.py:505
  30.1 0.6 copy-start.4
  44.7 64.2 %all-gather.5.cloned.1.call-start = ((), (), s32[]{:S(2)}) async-start(), calls=%async_computation.5 | async-start | bytes 5308416 | tf_op jit(solution)/shard_map/all_gather | solution.py:507
  45.4 40.4 %all-to-all-start.1 = ((bf16[64,80,128]{2,1,0:T(8,128)(2,1)}), bf16[64,80,128]{2,1,0:T(8,128)(2,1)S(1)}, u32[]{:S(2)}, u32[]{:S(2)}) async-start(bf16[64,80,128]{2,1,0:T(8,128)(2,1)} %bitcast.13), calls=%async_computation.1 | async-start | bytes 2621440 | tf_op jit(solution)/shard_map/all_to_all | solution.py:439
  85.8 45.2 %all-to-all-start.2 = ((bf16[64,80,128]{2,1,0:T(8,128)(2,1)}), bf16[64,80,128]{2,1,0:T(8,128)(2,1)S(1)}, u32[]{:S(2)}, u32[]{:S(2)}) async-start(bf16[64,80,128]{2,1,0:T(8,128)(2,1)} %bitcast.31), calls=%async_computation.2 | async-start | bytes 2621440 | tf_op jit(solution)/shard_map/all_to_all | solution.py:439
  108.9 2.3 %copy-start.11 = (bf16[18432,128]{1,0:T(8,128)(2,1)S(1)}, bf16[18432,128]{1,0:T(8,128)(2,1)}, u32[]{:S(2)}) copy-start(bf16[18432,128]{1,0:T(8,128)(2,1)} %all-gather.5.cloned.1.call-done.weight_ref) | copy-start | bytes 14155780
  113.3 1.3 copy-start
  114.5 1.1 copy-start.1
  115.7 1.2 copy-start.2
  139.1 49.0 %copy-start.5 = (s32[8,128]{1,0:T(8,128)S(1)}, s32[8,128]{1,0:T(8,128)}, u32[]{:S(2)}) copy-start(s32[8,128]{1,0:T(8,128)} %copy-done.4) | copy-start | bytes 12292
Sparse Core Ops, SparseCore 0:
  44.8 22.4 all-gather.2
  69.4 39.4 all-gather.4

commit v3 on v2

--- a/solution.py
+++ b/solution.py
@@ -95,7 +95,10 @@
 
 def segment_kernel(in_ref, out_ref, *, rows):
     count = in_ref.shape[0]
-    out_ref[0:count, :] = in_ref[:, 0 : 2 * LANES]
+    out_ref[0:count, 0:LANES] = in_ref[:, 0:LANES]
+    for i in range(0, count, LANES):
+        block = in_ref[i : i + LANES, LANES : 2 * LANES].astype(F32)
+        out_ref[i : i + LANES, LANES : 2 * LANES] = block.T.astype(BF16)
     tot = in_ref[:, 2 * LANES :].astype(F32)
     row, lane = iota(tot.shape, 0), iota(tot.shape, 1)
     line = jnp.sum(jnp.where(row == lane * rows, tot, 0.0), axis=0, keepdims=True)
@@ -146,18 +149,23 @@
 def attend_kernel(
     place_ref,
     lens_ref,
-    kv_ref,
-    query_ref,
-    hidden_ref,
-    proj_ref,
-    slot_ref,
+    kv_hbm,
+    query_hbm,
+    hidden_hbm,
+    proj_hbm,
+    slot_hbm,
     send_ref,
     max_ref,
     acc_ref,
+    line_buf,
     kv_buf,
+    query_ref,
+    hidden_ref,
     proj_buf,
+    slot_ref,
+    line_sem,
     kv_sem,
-    proj_sem,
+    other_sem,
     *,
     segments,
     rows,
@@ -166,24 +174,45 @@
     together,
 ):
     def kv_copy(b):
-        return pltpu.make_async_copy(kv_ref.at[b], kv_buf.at[b], kv_sem.at[b])
-
-    proj_copy = pltpu.make_async_copy(proj_ref, proj_buf, proj_sem)
+        at = pl.ds(0, rows)
+        return pltpu.make_async_copy(kv_hbm.at[b, at], kv_buf.at[b], kv_sem.at[b])
+
+    def line_copy(b):
+        at = pl.ds(rows, pitch - rows)
+        return pltpu.make_async_copy(kv_hbm.at[b, at], line_buf.at[b], line_sem.at[b])
+
+    query_copy, hidden_copy, proj_copy, slot_copy = [
+        pltpu.make_async_copy(src, dst, other_sem.at[i])
+        for i, (src, dst) in enumerate(
+            (
+                (query_hbm, query_ref),
+                (hidden_hbm, hidden_ref),
+                (proj_hbm, proj_buf),
+                (slot_hbm, slot_ref),
+            )
+        )
+    ]
+    for b in range(segments):
+        line_copy(b).start()
+    query_copy.start()
     for b in range(segments):
         kv_copy(b).start()
     proj_copy.start()
+    hidden_copy.start()
+    slot_copy.start()
     tokens = query_ref.shape[0]
     heads = query_ref.shape[1] // LANES
     scale = LANES**-0.5 * 1.4426950408889634
     max_ref[...] = jnp.full(max_ref.shape, NEG, F32)
     acc_ref[...] = jnp.zeros(acc_ref.shape, F32)
+    extra = acc_ref.shape[1] - LANES
     for b in range(segments):
-        kv_copy(b).wait()
+        line_copy(b).wait()
     seq, exp = place_ref[0], place_ref[1]
     total = jnp.zeros((16, LANES), F32)
     lane = iota((16, LANES), 1)
     for s in range(segments):
-        line = kv_buf[s, rows : rows + 16, 0:LANES].astype(F32)
+        line = line_buf[s, :, 0:LANES].astype(F32)
         take = jnp.logical_or(seq > s, jnp.logical_and(seq == s, lane < exp))
         total = total + jnp.where(take, line, 0.0)
     offset = (jnp.sum(total) * (1.0 / 16.0)).astype(jnp.int32)
@@ -192,45 +221,64 @@
         offset = offset + lens_ref[g]
         ends.append(offset)
     size = together * tokens
-    group = (iota((size, 1), 0) % tokens) // GROUP
-    limits = jnp.zeros((size, 1), jnp.int32)
+    group = (iota((1, size), 1) % tokens) // GROUP
+    limits = jnp.zeros((1, size), jnp.int32)
     for g, end in enumerate(ends):
         limits = jnp.where(group == g, end, limits)
-    ones = as_bf16(iota((rows, LANES), 1) == 0)
+    ones = jnp.ones((extra, rows), BF16)
 
     def block(masked):
         def body(b, carry):
-            keys = kv_buf[b, 0:rows, 0:LANES]
-            wide = jnp.concatenate([kv_buf[b, 0:rows, LANES : 2 * LANES], ones], axis=1)
-            for h in range(0, heads, together):
+            kv_copy(b).wait()
+            keys = kv_buf[b, :, 0:LANES]
+            values = jnp.concatenate(
+                [kv_buf[b, i : i + LANES, LANES : 2 * LANES] for i in range(0, rows, LANES)],
+                axis=1,
+            )
+            tall = jnp.concatenate([values, ones], axis=0)
+            for g in range(heads // together):
                 q = jnp.concatenate(
-                    [query_ref[:, i * LANES : (i + 1) * LANES] for i in range(h, h + together)],
+                    [
+                        query_ref[:, i * LANES : (i + 1) * LANES]
+                        for i in range(g * together, (g + 1) * together)
+                    ],
                     axis=0,
                 )
-                at = slice(h * tokens, h * tokens + size)
-                s = dot(q, keys, ((1,), (1,)))
+                s = dot(keys, q, ((1,), (1,)))
                 if masked:
-                    s = jnp.where(iota((size, rows), 1) + b * rows < limits, s, NEG)
-                old = max_ref[at, :]
-                new = jnp.maximum(old, jnp.max(s, axis=1, keepdims=True))
-                max_ref[at, :] = new
+                    s = jnp.where(iota((rows, size), 0) + b * rows < limits, s, NEG)
+                old = max_ref[g]
+                new = jnp.maximum(old, jnp.max(s, axis=0, keepdims=True))
+                max_ref[g] = new
                 w = jnp.exp2((s - new) * scale).astype(BF16)
                 factor = jnp.exp2((old - new) * scale)
-                acc_ref[at, :] = acc_ref[at, :] * factor + dot(w, wide)
+                acc_ref[g] = acc_ref[g] * factor + dot(tall, w)
             return carry
 
         return body
 
     full = ends[0] // rows
     last = (ends[-1] + rows - 1) // rows
+    query_copy.wait()
     lax.fori_loop(0, full, block(False), 0)
     lax.fori_loop(full, last, block(True), 0)
+
+    def unused(b, carry):
+        kv_copy(b).wait()
+        return carry
+
+    lax.fori_loop(last, segments, unused, 0)
     attended = []
-    for h in range(heads):
-        acc = acc_ref[h * tokens : (h + 1) * tokens, :]
-        attended.append((acc[:, :LANES] / acc[:, LANES : LANES + 1]).astype(BF16))
+    for g in range(heads // together):
+        acc = acc_ref[g]
+        part = (acc[:LANES, :] / acc[LANES : LANES + 1, :]).astype(BF16)
+        attended += [part[:, i * tokens : (i + 1) * tokens] for i in range(together)]
     proj_copy.wait()
-    mixed = hidden_ref[...].astype(F32) + dot(jnp.concatenate(attended, axis=1), proj_buf[...])
+    hidden_copy.wait()
+    slot_copy.wait()
+    mixed = hidden_ref[...].astype(F32) + dot(
+        jnp.concatenate(attended, axis=0), proj_buf[...], ((0,), (0,))
+    )
     chunks = hidden_ref.shape[1] // LANES
     slots = send_ref.shape[0] // chunks
     wide = dot(placed(slot_ref[...], top, slots), mixed.astype(BF16)).astype(BF16)
@@ -241,17 +289,9 @@
     fold_rows(wide, fold_matrix(BLOCK, chunks), store)
 
 
-def prepare_kernel(cot_ref, weight_ref, gate_ref, up_ref, back_ref, c_ref, *, shards, ff):
+def prepare_kernel(cot_ref, weight_ref, back_ref, c_ref, *, shards, ff):
     slots, width = c_ref.shape
     chunks = width // LANES
-    pitch = weight_ref.shape[0] // shards
-    for s in range(shards):
-        for i in range(ff // LANES):
-            for base, ref in ((0, gate_ref), (ff, up_ref)):
-                at = s * pitch + base + i * LANES
-                ref[s * LANES : (s + 1) * LANES, i * LANES : (i + 1) * LANES] = weight_ref[
-                    at : at + LANES, :
-                ]
     unfold_rows(
         lambda f, n: cot_ref[f : f + n, :], slots, chunks, unfold_matrix(BLOCK, chunks), c_ref
     )
@@ -259,10 +299,7 @@
     step = 256
     for j in range(ff // step):
         w_down = jnp.concatenate(
-            [
-                weight_ref[s * pitch + 2 * ff + j * step : s * pitch + 2 * ff + (j + 1) * step, :]
-                for s in range(shards)
-            ],
+            [weight_ref[s * ff + j * step : s * ff + (j + 1) * step, :] for s in range(shards)],
             axis=1,
         )
         back_ref[:, j * step : (j + 1) * step] = dot(c, w_down, ((1,), (1,)))
@@ -270,8 +307,7 @@
 
 def expert_kernel(
     row_ref,
-    gate_ref,
-    up_ref,
+    weight_ref,
     back_ref,
     out_ref,
     x_ref,
@@ -279,19 +315,26 @@
     gate_buf,
     up_buf,
     back_buf,
-    other_sem,
+    weight_sem,
+    back_sem,
     *,
     capacity,
 ):
     slots, width = x_ref.shape
     chunks = width // LANES
-    ff = gate_ref.shape[1]
-    others = [
-        pltpu.make_async_copy(src, dst, other_sem.at[i])
-        for i, (src, dst) in enumerate(
-            ((gate_ref, gate_buf), (up_ref, up_buf), (back_ref, back_buf))
-        )
-    ]
+    shards = weight_ref.shape[0]
+    rows = weight_ref.shape[1] // 2
+    ff = weight_ref.shape[2]
+    others = [pltpu.make_async_copy(back_ref, back_buf, back_sem)]
+    for s in range(shards):
+        for i, buf in enumerate((gate_buf, up_buf)):
+            others.append(
+                pltpu.make_async_copy(
+                    weight_ref.at[s, pl.ds(i * rows, rows)],
+                    buf.at[pl.ds(s * rows, rows)],
+                    weight_sem.at[s, i],
+                )
+            )
     for copy in others:
         copy.start()
     unfold_rows(
@@ -385,7 +428,7 @@
 
 
 HBM = pl.BlockSpec(memory_space=pltpu.HBM)
-TOGETHER = 2
+TOGETHER = 8
 
 
 def attend(place, lens, kv, queries, hidden, proj, slot_table, *, rows, slots):
@@ -398,15 +441,20 @@
             attend_kernel, segments=segments, rows=rows, pitch=pitch, top=top, together=TOGETHER
         ),
         out_shape=jax.ShapeDtypeStruct((slots * chunks, LANES), BF16),
-        in_specs=[SMEM, SMEM, HBM] + vmem(2) + [HBM] + vmem(1),
+        in_specs=[SMEM, SMEM] + [HBM] * 5,
         out_specs=vmem(1)[0],
         scratch_shapes=[
-            pltpu.VMEM((heads * tokens, 1), F32),
-            pltpu.VMEM((heads * tokens, 2 * LANES), F32),
-            pltpu.VMEM(kv.shape, BF16),
+            pltpu.VMEM((heads // TOGETHER, 1, TOGETHER * tokens), F32),
+            pltpu.VMEM((heads // TOGETHER, LANES + 16, TOGETHER * tokens), F32),
+            pltpu.VMEM((segments, pitch - rows, 2 * LANES), BF16),
+            pltpu.VMEM((segments, rows, 2 * LANES), BF16),
+            pltpu.VMEM(queries.shape, BF16),
+            pltpu.VMEM(hidden.shape, BF16),
             pltpu.VMEM(proj.shape, BF16),
+            pltpu.VMEM(slot_table.shape, jnp.int32),
             pltpu.SemaphoreType.DMA((segments,)),
-            pltpu.SemaphoreType.DMA(()),
+            pltpu.SemaphoreType.DMA((segments,)),
+            pltpu.SemaphoreType.DMA((4,)),
         ],
         compiler_params=params(58),
         cost_estimate=pl.CostEstimate(flops=0, bytes_accessed=0, transcendentals=0),
@@ -414,25 +462,27 @@
     )(place, lens, kv, queries, hidden, proj, slot_table)
 
 
-def expert(rows, gate, up, back, *, capacity):
-    slots, (width, ff) = back.shape[0], gate.shape
+def expert(rows, weights, back, *, capacity):
+    slots, (shards, pair, ff) = back.shape[0], weights.shape
+    width = shards * pair // 2
     chunks = width // LANES
     return pl.pallas_call(
         functools.partial(expert_kernel, capacity=capacity),
         out_shape=jax.ShapeDtypeStruct((slots // capacity, capacity * chunks + 8, LANES), BF16),
-        in_specs=vmem(1) + [HBM] * 3,
+        in_specs=vmem(1) + [HBM] * 2,
         out_specs=vmem(1)[0],
         scratch_shapes=[
             pltpu.VMEM((slots, width), BF16),
             pltpu.VMEM((slots, width), F32),
-            pltpu.VMEM(gate.shape, BF16),
-            pltpu.VMEM(up.shape, BF16),
+            pltpu.VMEM((width, ff), BF16),
+            pltpu.VMEM((width, ff), BF16),
             pltpu.VMEM(back.shape, F32),
-            pltpu.SemaphoreType.DMA((3,)),
+            pltpu.SemaphoreType.DMA((shards, 2)),
+            pltpu.SemaphoreType.DMA(()),
         ],
         compiler_params=params(50),
         name="expert",
-    )(rows, gate, up, back)
+    )(rows, weights, back)
 
 
 def exchange(rows):
@@ -497,14 +547,12 @@
         compiler_params=params(16),
         name="segment",
     )(kv_rows.reshape(rows, 3 * LANES))
-    def blocks(w):
-        return w[0].reshape(LANES, ff // LANES, LANES).transpose(1, 0, 2).reshape(ff, LANES)
-
-    shard = jnp.concatenate([blocks(w_gate), blocks(w_up), w_down[0]], axis=0)
-    segment, send_cot, shard = lax.optimization_barrier((segment, send_cot, shard))
+    down = lax.all_gather(w_down[0], "seq", axis=0, tiled=True)
+    shard = jnp.concatenate([w_gate[0], w_up[0]], axis=0)
+    segment, send_cot, shard, down = lax.optimization_barrier((segment, send_cot, shard, down))
     kv_all = lax.all_gather(segment, "seq", axis=0, tiled=True)
     recv_cot = exchange(send_cot.reshape(experts, each, LANES))
-    weights = lax.all_gather(shard, "seq", axis=0, tiled=True)
+    weights = lax.all_gather(shard, "seq", axis=0, tiled=False)
 
     send_rows = attend(
         place,
@@ -519,25 +567,20 @@
     )
     send_rows, recv_cot = lax.optimization_barrier((send_rows, recv_cot))
     recv_rows = exchange(send_rows.reshape(experts, each, LANES))
-    full_gate, full_up, down_back = pl.pallas_call(
+    down_back = pl.pallas_call(
         functools.partial(prepare_kernel, shards=shards, ff=ff),
-        out_shape=(
-            jax.ShapeDtypeStruct((width, ff), BF16),
-            jax.ShapeDtypeStruct((width, ff), BF16),
-            jax.ShapeDtypeStruct((slots, ff), F32),
-        ),
+        out_shape=jax.ShapeDtypeStruct((slots, ff), F32),
         in_specs=vmem(2),
-        out_specs=tuple(vmem(3)),
+        out_specs=vmem(1)[0],
         scratch_shapes=[pltpu.VMEM((slots, width), BF16)],
         compiler_params=params(24),
         cost_estimate=pl.CostEstimate(
             flops=40 * slots * width * ff, bytes_accessed=0, transcendentals=0
         ),
         name="prepare",
-    )(recv_cot.reshape(slots * chunks, LANES), weights)
-
+    )(recv_cot.reshape(slots * chunks, LANES), down)
     back = expert(
-        recv_rows.reshape(slots * chunks, LANES), full_gate, full_up, down_back, capacity=capacity
+        recv_rows.reshape(slots * chunks, LANES), weights, down_back, capacity=capacity
     )
     home = exchange(back)
 

time: 197 us -> 206 us (1.046)
  waiting for transfers between devices: 60.5 us -> 68.4 us
  starting transfers between devices: 31.5 us -> 37.2 us
  local copies, waits for them, and re-layouts: 9.28 us -> 6.72 us
  Pallas kernels: 30.9 us -> 28.4 us
    all_to_all x3, waiting for transfers between devices: 30.3 us -> 42.2 us  [exchange(): return lax.all_to_all(rows, 'exp', split_axis=0, concat_axis=0, tiled=True)]
    all_gather x1 -> x2, waiting for transfers between devices: 13.4 us -> 5.49 us  [the longest x1 5.49 us: local(): weights = lax.all_gather(shard, 'seq', axis=0, tiled=False)]
    all_to_all x3, starting transfers between devices: 31.4 us -> 37.1 us  [exchange(): return lax.all_to_all(rows, 'exp', split_axis=0, concat_axis=0, tiled=True)]
    all_gather x1, waiting for transfers between devices: 16.1 us -> 19.3 us  [local(): kv_all = lax.all_gather(segment, 'seq', axis=0, tiled=True)]
    pallas_call x1, Pallas kernels: 14.8 us -> 12.6 us  [attend(): pl.pallas_call(functools.partial(attend_kernel, segments=segments, rows=r...]
    unnamed x33 -> x29, local copies, waits for them, and re-layouts: 8.9 us -> 6.7 us
  transfers between devices with their start and end apart: 5 -> 6, of which waited for: 5 -> 5; matrix products, arithmetic and copies ran while one was open for 1% -> 1% of each run, Pallas kernels for 10% -> 9%
where the time goes in v3:
time: 206 us; the launch traced here: 205 us
  waiting for transfers between devices  68.4 us (33%)
  blocking collectives  49.4 us (24%)
  starting transfers between devices  37.2 us (18%)
  Pallas kernels  28.4 us (14%)
  between operations  13.9 us (7%)
  local copies, waits for them, and re-layouts  6.72 us (3%)
    all_to_all x1, blocking collectives, exchange(): return lax.all_to_all(rows, 'exp', split_axis=0, concat_axis=0, tiled=True)  49.4 us
    all_to_all x3, waiting for transfers between devices, exchange(): return lax.all_to_all(rows, 'exp', split_axis=0, concat_axis=0, tiled=True)  42.2 us
    all_to_all x3, starting transfers between devices, exchange(): return lax.all_to_all(rows, 'exp', split_axis=0, concat_axis=0, tiled=True)  37.1 us
    all_gather x1, waiting for transfers between devices, local(): kv_all = lax.all_gather(segment, 'seq', axis=0, tiled=True)  19.3 us
    pallas_call x1, Pallas kernels, attend(): pl.pallas_call(functools.partial(attend_kernel, segments=segments, rows=r...  12.6 us
    pallas_call x1, Pallas kernels, expert(): pl.pallas_call(functools.partial(expert_kernel, capacity=capacity), out_s...  8.29 us
    unnamed x29, local copies, waits for them, and re-layouts  6.7 us
    all_gather x1, waiting for transfers between devices, local(): weights = lax.all_gather(shard, 'seq', axis=0, tiled=False)  5.49 us
  transfers between devices with their start and end apart: 6, of which 5 were waited for; matrix products, arithmetic and copies ran while one was open for 1% of the time, Pallas kernels for 9%

profile of v3, /device:TPU:22, one launch (start us, length us, event | category | flops | bytes accessed | tf_op | source)
XLA Modules:
  0.0 205.4 jit_solution(12879971730914161604)
XLA Ops:
  7.2 0.0 all-gather.8.cloned.1.call-start
  7.2 0.7 all-gather.8.cloned.1.call-update
  7.9 0.7 copy-done.8
  8.6 0.7 copy-done.9
  9.3 0.7 copy-done.10
  9.9 1.3 pack.1
  11.3 16.5 %all-to-all-start = ((bf16[64,8,384]{2,1,0:T(8,128)(2,1)}), bf16[64,8,384]{2,1,0:T(8,128)(2,1)S(1)}, u32[]{:S(2)}, u32[]{:S(2)}) async-start(bf16[64,8,384]{2,1,0:T(8,128)(2,1)} %pack.1), calls=%async_computation | async-start | bytes 786432 | tf_op jit(solution)/shard_map/all_to_all | solution.py:489
  27.7 0.0 all-gather.6.cloned.1.call-start
  27.8 0.7 copy-done.4
  28.5 0.7 copy-done.6
  29.2 2.1 %dispatch.1 = (s32[8,128]{1,0:T(8,128)S(1)}, bf16[5120,128]{1,0:T(8,128)(2,1)}) custom-call(s32[4,128]{1,0:T(4,128)S(1)} %bitcast.22, bf16[4,128]{1,0:T(4,128)(2,1)S(1)} %bitcast.24, bf16[128,1024]{1,0:T(8,128)(2,1)S(1)} %copy-done.1), custom_call_target="tpu_custom_call" | custom-call | tf_op jit(solution)/shard_map/dispatch/pallas_call | solution.py:530
  31.3 0.6 copy-done.2
  31.9 0.8 pad_maximum_fusion
  32.7 11.7 %all-to-all-done = bf16[64,8,384]{2,1,0:T(8,128)(2,1)S(1)} async-done(((bf16[64,8,384]{2,1,0:T(8,128)(2,1)}), bf16[64,8,384]{2,1,0:T(8,128)(2,1)S(1)}, u32[]{:S(2)}, u32[]{:S(2)}) %all-to-all-start) | async-done | bytes 393248 | tf_op jit(solution)/shard_map/all_to_all | solution.py:489
  44.4 0.9 segment.1
  45.2 0.0 all-gather.6.cloned.1.call-update
  45.3 0.0 all-gather.10.cloned.1.call-start
  45.3 0.7 all-gather.10.cloned.1.call-update
  46.0 10.9 %all-to-all-start.1 = ((bf16[64,80,128]{2,1,0:T(8,128)(2,1)}), bf16[64,80,128]{2,1,0:T(8,128)(2,1)S(1)}, u32[]{:S(2)}, u32[]{:S(2)}) async-start(bf16[64,80,128]{2,1,0:T(8,128)(2,1)} %bitcast.9), calls=%async_computation.1 | async-start | bytes 2621440 | tf_op jit(solution)/shard_map/all_to_all | solution.py:489
  56.9 0.6 pad_add_fusion.place_ref
  57.5 19.3 %all-gather.6.cloned.1.call-done = bf16[4224,256]{1,0:T(8,128)(2,1)} async-done(((bf16[528,256]{1,0:T(8,128)(2,1)}), bf16[4224,256]{1,0:T(8,128)(2,1)}) %all-gather.6.cloned.1.call-update) | async-done | bytes 2162704 | tf_op jit(solution)/shard_map/all_gather | solution.py:553
  76.8 12.6 %attend.1 = bf16[5120,128]{1,0:T(8,128)(2,1)} custom-call(s32[2]{0:T(128)} %pad_add_fusion.place_ref, s32[4]{0:T(128)} %lens_ref.3, bf16[8,528,256]{2,1,0:T(8,128)(2,1)} %bitcast.29, bf16[128,1024]{1,0:T(8,128)(2,1)} %query_hbm.1, bf16[128,1024]{1,0:T(8,128)(2,1)} %hidden_hbm.1, bf16[1024,1024]{1,0:T(8,128)(2,1)} %proj_hbm.1, s32[8,128]{1,0:T(8,128)} %copy-done.2), custom_call_target="tpu_custom_call" | custom-call | tf_op jit(solution)/shard_map/attend/pallas_call | solution.py:439
  89.3 3.7 %all-to-all-done.1 = bf16[64,80,128]{2,1,0:T(8,128)(2,1)S(1)} async-done(((bf16[64,80,128]{2,1,0:T(8,128)(2,1)}), bf16[64,80,128]{2,1,0:T(8,128)(2,1)S(1)}, u32[]{:S(2)}, u32[]{:S(2)}) %all-to-all-start.1) | async-done | bytes 1310752 | tf_op jit(solution)/shard_map/all_to_all | solution.py:489
  93.0 9.7 %all-to-all-start.2 = ((bf16[64,80,128]{2,1,0:T(8,128)(2,1)}), bf16[64,80,128]{2,1,0:T(8,128)(2,1)S(1)}, u32[]{:S(2)}, u32[]{:S(2)}) async-start(bf16[64,80,128]{2,1,0:T(8,128)(2,1)} %bitcast.27), calls=%async_computation.2 | async-start | bytes 2621440 | tf_op jit(solution)/shard_map/all_to_all | solution.py:489
  102.7 1.4 copy-done.11
  104.2 1.6 prepare.1.back_ref
  105.8 1.3 copy-done
  107.1 5.5 %all-gather.10.cloned.1.call-done = bf16[2048,768]{1,0:T(8,128)(2,1)} async-done(((bf16[256,768]{1,0:T(8,128)(2,1)}), bf16[2048,768]{1,0:T(8,128)(2,1)}) %all-gather.10.cloned.1.call-update) | async-done | bytes 3145744 | tf_op jit(solution)/shard_map/all_gather | solution.py:555
  112.6 26.8 %all-to-all-done.2 = bf16[64,80,128]{2,1,0:T(8,128)(2,1)S(1)} async-done(((bf16[64,80,128]{2,1,0:T(8,128)(2,1)}), bf16[64,80,128]{2,1,0:T(8,128)(2,1)S(1)}, u32[]{:S(2)}, u32[]{:S(2)}) %all-to-all-start.2) | async-done | bytes 1310752 | tf_op jit(solution)/shard_map/all_to_all | solution.py:489
  139.4 8.3 %expert.1 = bf16[64,88,128]{2,1,0:T(8,128)(2,1)S(1)} custom-call(bf16[5120,128]{1,0:T(8,128)(2,1)S(1)} %bitcast.18, bf16[8,256,768]{2,1,0:T(8,128)(2,1)} %bitcast.28, f32[640,768]{1,0:T(8,128)} %copy-done), custom_call_target="tpu_custom_call" | custom-call | tf_op jit(solution)/shard_map/expert/pallas_call | solution.py:469
  147.7 49.4 %all_to_all.20.back_ref = bf16[64,88,128]{2,1,0:T(8,128)(2,1)S(1)} all-to-all(bf16[64,88,128]{2,1,0:T(8,128)(2,1)S(1)} %expert.1), channel_id=1, replica_groups=mesh['seq'=8,'exp'=64] {'exp'}, dimensions={0} | all-to-all | bytes 2883584 | tf_op jit(solution)/shard_map/all_to_all | solution.py:489
  197.2 1.6 combine.1
  (23 shorter events, 0.1 us)
Async XLA Ops:
  7.2 20.6 %copy-start.1 = (bf16[128,1024]{1,0:T(8,128)(2,1)S(1)}, bf16[128,1024]{1,0:T(8,128)(2,1)}, u32[]{:S(2)}) copy-start(bf16[128,1024]{1,0:T(8,128)(2,1)} %cot_ref.1) | copy-start | bytes 786436
  7.2 38.1 %all-gather.8.cloned.1.call-start = ((), (), s32[]{:S(2)}) async-start(), calls=%async_computation.5 | async-start | bytes 1769472 | tf_op jit(solution)/shard_map/all_gather | solution.py:550
  7.9 0.7 copy-start.8
  8.6 0.7 copy-start.9
  9.3 0.7 copy-start.10
  9.9 22.0 %copy-start.12 = (bf16[1,128,768]{2,1,0:T(8,128)(2,1)S(1)}, bf16[1,128,768]{2,1,0:T(8,128)(2,1)}, u32[]{:S(2)}) copy-start(bf16[1,128,768]{2,1,0:T(8,128)(2,1)} %param.21) | copy-start | bytes 589828
  9.9 22.0 %copy-start.13 = (bf16[1,128,768]{2,1,0:T(8,128)(2,1)S(1)}, bf16[1,128,768]{2,1,0:T(8,128)(2,1)}, u32[]{:S(2)}) copy-start(bf16[1,128,768]{2,1,0:T(8,128)(2,1)} %param.20) | copy-start | bytes 589828
  11.3 33.1 %all-to-all-start = ((bf16[64,8,384]{2,1,0:T(8,128)(2,1)}), bf16[64,8,384]{2,1,0:T(8,128)(2,1)S(1)}, u32[]{:S(2)}, u32[]{:S(2)}) async-start(bf16[64,8,384]{2,1,0:T(8,128)(2,1)} %pack.1), calls=%async_computation | async-start | bytes 786432 | tf_op jit(solution)/shard_map/all_to_all | solution.py:489
  27.7 49.0 %all-gather.6.cloned.1.call-start = ((), (), s32[]{:S(2)}) async-start(), calls=%async_computation.4 | async-start | bytes 2433024 | tf_op jit(solution)/shard_map/all_gather | solution.py:553
  27.8 0.7 copy-start.4
  28.5 0.7 copy-start.6
  31.3 0.6 copy-start.2
  45.3 67.3 %all-gather.10.cloned.1.call-start = ((), (), s32[]{:S(2)}) async-start(), calls=%async_computation.6 | async-start | bytes 3538944 | tf_op jit(solution)/shard_map/all_gather | solution.py:555
  46.0 47.0 %all-to-all-start.1 = ((bf16[64,80,128]{2,1,0:T(8,128)(2,1)}), bf16[64,80,128]{2,1,0:T(8,128)(2,1)S(1)}, u32[]{:S(2)}, u32[]{:S(2)}) async-start(bf16[64,80,128]{2,1,0:T(8,128)(2,1)} %bitcast.9), calls=%async_computation.1 | async-start | bytes 2621440 | tf_op jit(solution)/shard_map/all_to_all | solution.py:489
  93.0 46.4 %all-to-all-start.2 = ((bf16[64,80,128]{2,1,0:T(8,128)(2,1)}), bf16[64,80,128]{2,1,0:T(8,128)(2,1)S(1)}, u32[]{:S(2)}, u32[]{:S(2)}) async-start(bf16[64,80,128]{2,1,0:T(8,128)(2,1)} %bitcast.27), calls=%async_computation.2 | async-start | bytes 2621440 | tf_op jit(solution)/shard_map/all_to_all | solution.py:489
  102.7 1.4 copy-start.11
  105.8 1.3 copy-start
  147.7 49.5 %copy-start.3 = (s32[8,128]{1,0:T(8,128)S(1)}, s32[8,128]{1,0:T(8,128)}, u32[]{:S(2)}) copy-start(s32[8,128]{1,0:T(8,128)} %copy-done.2) | copy-start | bytes 12292
  147.7 49.5 %copy-start.5 = (s32[128,4]{0,1:T(4,128)S(1)}, s32[128,4]{0,1:T(4,128)}, u32[]{:S(2)}) copy-start(s32[128,4]{0,1:T(4,128)} %param.18) | copy-start | bytes 6148
  147.7 49.5 %copy-start.7 = (bf16[128,4]{0,1:T(4,128)(2,1)S(1)}, bf16[128,4]{0,1:T(4,128)(2,1)}, u32[]{:S(2)}) copy-start(bf16[128,4]{0,1:T(4,128)(2,1)} %param.19) | copy-start | bytes 3076
Sparse Core Ops, SparseCore 0:
  10.1 32.5 all-gather.7
  45.5 31.2 all-gather.5
  78.9 33.6 all-gather.9

commit v4 on v3

--- a/solution.py
+++ b/solution.py
@@ -82,15 +82,23 @@
                 ] = out[c * BLOCK : (c + 1) * BLOCK, half * LANES : (half + 1) * LANES]
 
 
-def pack_kernel(lens_ref, key_ref, value_ref, out_ref):
-    copies = out_ref.shape[0]
+def pack_kernel(lens_ref, key_hbm, value_hbm, out_ref, key_ref, value_ref, sem):
+    copies = [
+        pltpu.make_async_copy(key_hbm, key_ref, sem.at[0]),
+        pltpu.make_async_copy(value_hbm, value_ref, sem.at[1]),
+    ]
+    for copy in copies:
+        copy.start()
+    copies_out = out_ref.shape[0]
     total = lens_ref[0]
     for i in range(1, lens_ref.shape[0]):
         total = total + lens_ref[i]
     rows = key_ref.shape[0]
     tot = jnp.full((rows, LANES), total.astype(F32), F32).astype(BF16)
+    for copy in copies:
+        copy.wait()
     one = jnp.concatenate([key_ref[...], value_ref[...], tot], axis=1)
-    out_ref[...] = jnp.broadcast_to(one[None], (copies,) + one.shape)
+    out_ref[...] = jnp.broadcast_to(one[None], (copies_out,) + one.shape)
 
 
 def segment_kernel(in_ref, out_ref, *, rows):
@@ -289,20 +297,36 @@
     fold_rows(wide, fold_matrix(BLOCK, chunks), store)
 
 
-def prepare_kernel(cot_ref, weight_ref, back_ref, c_ref, *, shards, ff):
+def prepare_kernel(cot_ref, weight_ref, back_ref, c_ref, down_buf, down_sem):
     slots, width = c_ref.shape
     chunks = width // LANES
+    shards, _, ff = down_buf.shape
+    copies = [
+        pltpu.make_async_copy(
+            weight_ref.at[s, pl.ds(2 * LANES, LANES)], down_buf.at[s], down_sem.at[s]
+        )
+        for s in range(shards)
+    ]
+    for copy in copies:
+        copy.start()
     unfold_rows(
         lambda f, n: cot_ref[f : f + n, :], slots, chunks, unfold_matrix(BLOCK, chunks), c_ref
     )
     c = c_ref[...]
+    for copy in copies:
+        copy.wait()
     step = 256
-    for j in range(ff // step):
+    for j in range(0, ff, step):
         w_down = jnp.concatenate(
-            [weight_ref[s * ff + j * step : s * ff + (j + 1) * step, :] for s in range(shards)],
+            [
+                jnp.concatenate(
+                    [down_buf[s, :, i : i + LANES] for i in range(j, j + step, LANES)], axis=0
+                )
+                for s in range(shards)
+            ],
             axis=1,
         )
-        back_ref[:, j * step : (j + 1) * step] = dot(c, w_down, ((1,), (1,)))
+        back_ref[:, j : j + step] = dot(c, w_down, ((1,), (1,)))
 
 
 def expert_kernel(
@@ -323,7 +347,7 @@
     slots, width = x_ref.shape
     chunks = width // LANES
     shards = weight_ref.shape[0]
-    rows = weight_ref.shape[1] // 2
+    rows = gate_buf.shape[0] // shards
     ff = weight_ref.shape[2]
     others = [pltpu.make_async_copy(back_ref, back_buf, back_sem)]
     for s in range(shards):
@@ -463,8 +487,8 @@
 
 
 def expert(rows, weights, back, *, capacity):
-    slots, (shards, pair, ff) = back.shape[0], weights.shape
-    width = shards * pair // 2
+    slots, (shards, _, ff) = back.shape[0], weights.shape
+    width = shards * LANES
     chunks = width // LANES
     return pl.pallas_call(
         functools.partial(expert_kernel, capacity=capacity),
@@ -520,9 +544,14 @@
     packed = pl.pallas_call(
         pack_kernel,
         out_shape=jax.ShapeDtypeStruct((experts, own_rows, 3 * LANES), BF16),
-        in_specs=[SMEM] + vmem(2),
+        in_specs=[SMEM, HBM, HBM],
         out_specs=vmem(1)[0],
-        compiler_params=params(16),
+        scratch_shapes=[
+            pltpu.VMEM(thinker_keys.shape, BF16),
+            pltpu.VMEM(thinker_values.shape, BF16),
+            pltpu.SemaphoreType.DMA((2,)),
+        ],
+        compiler_params=params(58),
         name="pack",
     )(thinker_lengths, thinker_keys, thinker_values)
     kv_rows = exchange(packed)
@@ -547,9 +576,11 @@
         compiler_params=params(16),
         name="segment",
     )(kv_rows.reshape(rows, 3 * LANES))
-    down = lax.all_gather(w_down[0], "seq", axis=0, tiled=True)
-    shard = jnp.concatenate([w_gate[0], w_up[0]], axis=0)
-    segment, send_cot, shard, down = lax.optimization_barrier((segment, send_cot, shard, down))
+    lower = jnp.concatenate(
+        [w_down[0][i * LANES : (i + 1) * LANES, :] for i in range(ff // LANES)], axis=1
+    )
+    shard = jnp.concatenate([w_gate[0], w_up[0], lower], axis=0)
+    segment, send_cot, shard = lax.optimization_barrier((segment, send_cot, shard))
     kv_all = lax.all_gather(segment, "seq", axis=0, tiled=True)
     recv_cot = exchange(send_cot.reshape(experts, each, LANES))
     weights = lax.all_gather(shard, "seq", axis=0, tiled=False)
@@ -568,17 +599,21 @@
     send_rows, recv_cot = lax.optimization_barrier((send_rows, recv_cot))
     recv_rows = exchange(send_rows.reshape(experts, each, LANES))
     down_back = pl.pallas_call(
-        functools.partial(prepare_kernel, shards=shards, ff=ff),
+        prepare_kernel,
         out_shape=jax.ShapeDtypeStruct((slots, ff), F32),
-        in_specs=vmem(2),
+        in_specs=[vmem(1)[0], HBM],
         out_specs=vmem(1)[0],
-        scratch_shapes=[pltpu.VMEM((slots, width), BF16)],
-        compiler_params=params(24),
+        scratch_shapes=[
+            pltpu.VMEM((slots, width), BF16),
+            pltpu.VMEM((shards, LANES, ff), BF16),
+            pltpu.SemaphoreType.DMA((shards,)),
+        ],
+        compiler_params=params(50),
         cost_estimate=pl.CostEstimate(
             flops=40 * slots * width * ff, bytes_accessed=0, transcendentals=0
         ),
         name="prepare",
-    )(recv_cot.reshape(slots * chunks, LANES), down)
+    )(recv_cot.reshape(slots * chunks, LANES), weights)
     back = expert(
         recv_rows.reshape(slots * chunks, LANES), weights, down_back, capacity=capacity
     )

time: 206 us -> 196 us (0.951)
  starting transfers between devices: 37.2 us -> 29.1 us
  local copies, waits for them, and re-layouts: 6.72 us -> 3.56 us
  Pallas kernels: 28.4 us -> 30.9 us
    all_gather x1, waiting for transfers between devices: 5.49 us -> 15.6 us  [local(): weights = lax.all_gather(shard, 'seq', axis=0, tiled=False)]
    all_to_all x3, waiting for transfers between devices: 42.2 us -> 34.1 us  [exchange(): return lax.all_to_all(rows, 'exp', split_axis=0, concat_axis=0, tiled=True)]
    all_to_all x3, starting transfers between devices: 37.1 us -> 29.1 us  [exchange(): return lax.all_to_all(rows, 'exp', split_axis=0, concat_axis=0, tiled=True)]
    all_gather x1, waiting for transfers between devices: 19.3 us -> 16 us  [local(): kv_all = lax.all_gather(segment, 'seq', axis=0, tiled=True)]
    unnamed x29 -> x24, local copies, waits for them, and re-layouts: 6.7 us -> 3.53 us
  transfers between devices with their start and end apart: 6 -> 5, of which waited for: 5 -> 5; matrix products, arithmetic and copies ran while one was open for 1% -> 2% of each run, Pallas kernels for 9% -> 9%
where the time goes in v4:
time: 196 us; the launch traced here: 195 us
  waiting for transfers between devices  66.5 us (34%)
  blocking collectives  49.2 us (25%)
  Pallas kernels  30.9 us (16%)
  starting transfers between devices  29.1 us (15%)
  between operations  14.2 us (7%)
  local copies, waits for them, and re-layouts  3.56 us (2%)
    all_to_all x1, blocking collectives, exchange(): return lax.all_to_all(rows, 'exp', split_axis=0, concat_axis=0, tiled=True)  49.2 us
    all_to_all x3, waiting for transfers between devices, exchange(): return lax.all_to_all(rows, 'exp', split_axis=0, concat_axis=0, tiled=True)  34.1 us
    all_to_all x3, starting transfers between devices, exchange(): return lax.all_to_all(rows, 'exp', split_axis=0, concat_axis=0, tiled=True)  29.1 us
    all_gather x1, waiting for transfers between devices, local(): kv_all = lax.all_gather(segment, 'seq', axis=0, tiled=True)  16 us
    all_gather x1, waiting for transfers between devices, local(): weights = lax.all_gather(shard, 'seq', axis=0, tiled=False)  15.6 us
    pallas_call x1, Pallas kernels, attend(): pl.pallas_call(functools.partial(attend_kernel, segments=segments, rows=r...  12.6 us
    pallas_call x1, Pallas kernels, expert(): pl.pallas_call(functools.partial(expert_kernel, capacity=capacity), out_s...  8.3 us
  transfers between devices with their start and end apart: 5, of which 5 were waited for; matrix products, arithmetic and copies ran while one was open for 2% of the time, Pallas kernels for 9%

profile of v4, /device:TPU:22, one launch (start us, length us, event | category | flops | bytes accessed | tf_op | source)
XLA Modules:
  0.0 195.0 jit_solution(9221636168179690284)
XLA Ops:
  7.2 0.0 copy-start.8
  7.2 0.0 copy-start.1
  7.2 0.0 copy-start.5
  7.2 0.0 copy-start.4
  7.2 0.0 copy-start.6
  7.2 0.0 copy-start.7
  7.2 2.3 %pack.1 = bf16[64,8,384]{2,1,0:T(8,128)(2,1)} custom-call(s32[4]{0:T(128)} %lens_ref.3, bf16[8,128]{1,0:T(8,128)(2,1)} %key_hbm.1, bf16[8,128]{1,0:T(8,128)(2,1)} %value_hbm.1), custom_call_target="tpu_custom_call" | custom-call | tf_op jit(solution)/shard_map/pack/pallas_call | solution.py:544
  9.5 16.5 %all-to-all-start = ((bf16[64,8,384]{2,1,0:T(8,128)(2,1)}), bf16[64,8,384]{2,1,0:T(8,128)(2,1)S(1)}, u32[]{:S(2)}, u32[]{:S(2)}) async-start(bf16[64,8,384]{2,1,0:T(8,128)(2,1)} %pack.1), calls=%async_computation | async-start | bytes 786432 | tf_op jit(solution)/shard_map/all_to_all | solution.py:513
  26.0 0.0 all-gather.4.cloned.1.call-start
  26.1 0.8 bitcast_dynamic-update-slice_fusion.5
  26.8 0.8 bitcast_dynamic-update-slice_fusion.4
  27.7 2.1 %dispatch.1 = (s32[8,128]{1,0:T(8,128)S(1)}, bf16[5120,128]{1,0:T(8,128)(2,1)}) custom-call(s32[4,128]{1,0:T(4,128)S(1)} %bitcast.33, bf16[4,128]{1,0:T(4,128)(2,1)S(1)} %bitcast.35, bf16[128,1024]{1,0:T(8,128)(2,1)S(1)} %copy-done.1), custom_call_target="tpu_custom_call" | custom-call | tf_op jit(solution)/shard_map/dispatch/pallas_call | solution.py:559
  29.8 0.6 copy-done.2
  30.4 0.9 pad_maximum_fusion
  31.3 11.4 %all-to-all-done = bf16[64,8,384]{2,1,0:T(8,128)(2,1)S(1)} async-done(((bf16[64,8,384]{2,1,0:T(8,128)(2,1)}), bf16[64,8,384]{2,1,0:T(8,128)(2,1)S(1)}, u32[]{:S(2)}, u32[]{:S(2)}) %all-to-all-start) | async-done | bytes 393248 | tf_op jit(solution)/shard_map/all_to_all | solution.py:513
  42.7 0.9 segment.1
  43.5 0.0 all-gather.4.cloned.1.call-update
  43.5 0.0 all-gather.6.cloned.1.call-start
  43.6 0.7 all-gather.6.cloned.1.call-update
  44.3 5.2 %all-to-all-start.1 = ((bf16[64,80,128]{2,1,0:T(8,128)(2,1)}), bf16[64,80,128]{2,1,0:T(8,128)(2,1)S(1)}, u32[]{:S(2)}, u32[]{:S(2)}) async-start(bf16[64,80,128]{2,1,0:T(8,128)(2,1)} %bitcast.14), calls=%async_computation.1 | async-start | bytes 2621440 | tf_op jit(solution)/shard_map/all_to_all | solution.py:513
  49.5 0.6 pad_add_fusion.place_ref
  50.1 16.0 %all-gather.4.cloned.1.call-done = bf16[4224,256]{1,0:T(8,128)(2,1)} async-done(((bf16[528,256]{1,0:T(8,128)(2,1)}), bf16[4224,256]{1,0:T(8,128)(2,1)}) %all-gather.4.cloned.1.call-update) | async-done | bytes 2162704 | tf_op jit(solution)/shard_map/all_gather | solution.py:584
  66.1 12.6 %attend.1 = bf16[5120,128]{1,0:T(8,128)(2,1)} custom-call(s32[2]{0:T(128)} %pad_add_fusion.place_ref, s32[4]{0:T(128)} %lens_ref.3, bf16[8,528,256]{2,1,0:T(8,128)(2,1)} %bitcast.40, bf16[128,1024]{1,0:T(8,128)(2,1)} %query_hbm.1, bf16[128,1024]{1,0:T(8,128)(2,1)} %hidden_hbm.1, bf16[1024,1024]{1,0:T(8,128)(2,1)} %proj_hbm.1, s32[8,128]{1,0:T(8,128)} %copy-done.2), custom_call_target="tpu_custom_call" | custom-call | tf_op jit(solution)/shard_map/attend/pallas_call | solution.py:463
  78.7 6.0 %all-to-all-done.1 = bf16[64,80,128]{2,1,0:T(8,128)(2,1)S(1)} async-done(((bf16[64,80,128]{2,1,0:T(8,128)(2,1)}), bf16[64,80,128]{2,1,0:T(8,128)(2,1)S(1)}, u32[]{:S(2)}, u32[]{:S(2)}) %all-to-all-start.1) | async-done | bytes 1310752 | tf_op jit(solution)/shard_map/all_to_all | solution.py:513
  84.7 7.4 %all-to-all-start.2 = ((bf16[64,80,128]{2,1,0:T(8,128)(2,1)}), bf16[64,80,128]{2,1,0:T(8,128)(2,1)S(1)}, u32[]{:S(2)}, u32[]{:S(2)}) async-start(bf16[64,80,128]{2,1,0:T(8,128)(2,1)} %bitcast.37), calls=%async_computation.2 | async-start | bytes 2621440 | tf_op jit(solution)/shard_map/all_to_all | solution.py:513
  92.1 15.6 %all-gather.6.cloned.1.call-done = bf16[3072,768]{1,0:T(8,128)(2,1)} async-done(((bf16[384,768]{1,0:T(8,128)(2,1)}), bf16[3072,768]{1,0:T(8,128)(2,1)}) %all-gather.6.cloned.1.call-update) | async-done | bytes 4718608 | tf_op jit(solution)/shard_map/all_gather | solution.py:586
  107.8 3.1 %prepare.1.back_ref = f32[640,768]{1,0:T(8,128)S(1)} custom-call(bf16[5120,128]{1,0:T(8,128)(2,1)S(1)} %bitcast.31, bf16[8,384,768]{2,1,0:T(8,128)(2,1)} %bitcast.38), custom_call_target="tpu_custom_call" | custom-call | flops 20132659200 | tf_op jit(solution)/shard_map/prepare/pallas_call | solution.py:601
  110.9 1.3 copy-done
  112.2 16.7 %all-to-all-done.2 = bf16[64,80,128]{2,1,0:T(8,128)(2,1)S(1)} async-done(((bf16[64,80,128]{2,1,0:T(8,128)(2,1)}), bf16[64,80,128]{2,1,0:T(8,128)(2,1)S(1)}, u32[]{:S(2)}, u32[]{:S(2)}) %all-to-all-start.2) | async-done | bytes 1310752 | tf_op jit(solution)/shard_map/all_to_all | solution.py:513
  128.9 8.3 %expert.1 = bf16[64,88,128]{2,1,0:T(8,128)(2,1)S(1)} custom-call(bf16[5120,128]{1,0:T(8,128)(2,1)S(1)} %bitcast.29, bf16[8,384,768]{2,1,0:T(8,128)(2,1)} %bitcast.39, f32[640,768]{1,0:T(8,128)} %copy-done), custom_call_target="tpu_custom_call" | custom-call | tf_op jit(solution)/shard_map/expert/pallas_call | solution.py:493
  137.2 49.2 %all_to_all.20.back_ref = bf16[64,88,128]{2,1,0:T(8,128)(2,1)S(1)} all-to-all(bf16[64,88,128]{2,1,0:T(8,128)(2,1)S(1)} %expert.1), channel_id=1, replica_groups=mesh['seq'=8,'exp'=64] {'exp'}, dimensions={0} | all-to-all | bytes 2883584 | tf_op jit(solution)/shard_map/all_to_all | solution.py:513
  186.5 1.7 combine.1
  (16 shorter events, 0.1 us)
Async XLA Ops:
  7.2 20.4 %copy-start.8 = (bf16[1,768,128]{2,1,0:T(8,128)(2,1)S(1)}, bf16[1,768,128]{2,1,0:T(8,128)(2,1)}, u32[]{:S(2)}) copy-start(bf16[1,768,128]{2,1,0:T(8,128)(2,1)} %param.22) | copy-start | bytes 589828
  7.2 20.5 %copy-start.1 = (bf16[128,1024]{1,0:T(8,128)(2,1)S(1)}, bf16[128,1024]{1,0:T(8,128)(2,1)}, u32[]{:S(2)}) copy-start(bf16[128,1024]{1,0:T(8,128)(2,1)} %cot_ref.1) | copy-start | bytes 786436
  7.2 20.5 %copy-start.5 = (bf16[128,4]{0,1:T(4,128)(2,1)S(1)}, bf16[128,4]{0,1:T(4,128)(2,1)}, u32[]{:S(2)}) copy-start(bf16[128,4]{0,1:T(4,128)(2,1)} %param.19) | copy-start | bytes 3076
  7.2 20.5 %copy-start.4 = (s32[128,4]{0,1:T(4,128)S(1)}, s32[128,4]{0,1:T(4,128)}, u32[]{:S(2)}) copy-start(s32[128,4]{0,1:T(4,128)} %param.18) | copy-start | bytes 6148
  7.2 23.2 %copy-start.6 = (bf16[1,128,768]{2,1,0:T(8,128)(2,1)S(1)}, bf16[1,128,768]{2,1,0:T(8,128)(2,1)}, u32[]{:S(2)}) copy-start(bf16[1,128,768]{2,1,0:T(8,128)(2,1)} %param.21) | copy-start | bytes 589828
  7.2 23.2 %copy-start.7 = (bf16[1,128,768]{2,1,0:T(8,128)(2,1)S(1)}, bf16[1,128,768]{2,1,0:T(8,128)(2,1)}, u32[]{:S(2)}) copy-start(bf16[1,128,768]{2,1,0:T(8,128)(2,1)} %param.20) | copy-start | bytes 589828
  9.5 33.1 %all-to-all-start = ((bf16[64,8,384]{2,1,0:T(8,128)(2,1)}), bf16[64,8,384]{2,1,0:T(8,128)(2,1)S(1)}, u32[]{:S(2)}, u32[]{:S(2)}) async-start(bf16[64,8,384]{2,1,0:T(8,128)(2,1)} %pack.1), calls=%async_computation | async-start | bytes 786432 | tf_op jit(solution)/shard_map/all_to_all | solution.py:513
  26.0 40.1 %all-gather.4.cloned.1.call-start = ((), (), s32[]{:S(2)}) async-start(), calls=%async_computation.4 | async-start | bytes 2433024 | tf_op jit(solution)/shard_map/all_gather | solution.py:584
  29.8 0.6 copy-start.2
  43.5 64.2 %all-gather.6.cloned.1.call-start = ((), (), s32[]{:S(2)}) async-start(), calls=%async_computation.5 | async-start | bytes 5308416 | tf_op jit(solution)/shard_map/all_gather | solution.py:586
  44.3 40.4 %all-to-all-start.1 = ((bf16[64,80,128]{2,1,0:T(8,128)(2,1)}), bf16[64,80,128]{2,1,0:T(8,128)(2,1)S(1)}, u32[]{:S(2)}, u32[]{:S(2)}) async-start(bf16[64,80,128]{2,1,0:T(8,128)(2,1)} %bitcast.14), calls=%async_computation.1 | async-start | bytes 2621440 | tf_op jit(solution)/shard_map/all_to_all | solution.py:513
  84.7 44.2 %all-to-all-start.2 = ((bf16[64,80,128]{2,1,0:T(8,128)(2,1)}), bf16[64,80,128]{2,1,0:T(8,128)(2,1)S(1)}, u32[]{:S(2)}, u32[]{:S(2)}) async-start(bf16[64,80,128]{2,1,0:T(8,128)(2,1)} %bitcast.37), calls=%async_computation.2 | async-start | bytes 2621440 | tf_op jit(solution)/shard_map/all_to_all | solution.py:513
  110.9 1.3 copy-start
  137.2 49.3 %copy-start.3 = (s32[8,128]{1,0:T(8,128)S(1)}, s32[8,128]{1,0:T(8,128)}, u32[]{:S(2)}) copy-start(s32[8,128]{1,0:T(8,128)} %copy-done.2) | copy-start | bytes 12292
Sparse Core Ops, SparseCore 0:
  43.7 22.4 all-gather.3
  68.3 39.4 all-gather.5

commit v5 on v4

--- a/solution.py
+++ b/solution.py
@@ -236,14 +236,17 @@
     ones = jnp.ones((extra, rows), BF16)
 
     def block(masked):
-        def body(b, carry):
-            kv_copy(b).wait()
-            keys = kv_buf[b, :, 0:LANES]
-            values = jnp.concatenate(
-                [kv_buf[b, i : i + LANES, LANES : 2 * LANES] for i in range(0, rows, LANES)],
-                axis=1,
-            )
-            tall = jnp.concatenate([values, ones], axis=0)
+        def body(step, carry):
+            keys, talls = [], []
+            for i in range(SUB):
+                b = step * SUB + i
+                kv_copy(b).wait()
+                keys.append(kv_buf[b, :, 0:LANES])
+                values = jnp.concatenate(
+                    [kv_buf[b, r : r + LANES, LANES : 2 * LANES] for r in range(0, rows, LANES)],
+                    axis=1,
+                )
+                talls.append(jnp.concatenate([values, ones], axis=0))
             for g in range(heads // together):
                 q = jnp.concatenate(
                     [
@@ -252,21 +255,27 @@
                     ],
                     axis=0,
                 )
-                s = dot(keys, q, ((1,), (1,)))
-                if masked:
-                    s = jnp.where(iota((rows, size), 0) + b * rows < limits, s, NEG)
                 old = max_ref[g]
-                new = jnp.maximum(old, jnp.max(s, axis=0, keepdims=True))
+                new, scores = old, []
+                for i in range(SUB):
+                    s = dot(keys[i], q, ((1,), (1,)))
+                    if masked:
+                        place = iota((rows, size), 0) + (step * SUB + i) * rows
+                        s = jnp.where(place < limits, s, NEG)
+                    new = jnp.maximum(new, jnp.max(s, axis=0, keepdims=True))
+                    scores.append(s)
                 max_ref[g] = new
-                w = jnp.exp2((s - new) * scale).astype(BF16)
-                factor = jnp.exp2((old - new) * scale)
-                acc_ref[g] = acc_ref[g] * factor + dot(tall, w)
+                acc = acc_ref[g] * jnp.exp2((old - new) * scale)
+                for i in range(SUB):
+                    w = jnp.exp2((scores[i] - new) * scale).astype(BF16)
+                    acc = acc + dot(talls[i], w)
+                acc_ref[g] = acc
             return carry
 
         return body
 
-    full = ends[0] // rows
-    last = (ends[-1] + rows - 1) // rows
+    full = ends[0] // (rows * SUB)
+    last = (ends[-1] + rows * SUB - 1) // (rows * SUB)
     query_copy.wait()
     lax.fori_loop(0, full, block(False), 0)
     lax.fori_loop(full, last, block(True), 0)
@@ -275,7 +284,7 @@
         kv_copy(b).wait()
         return carry
 
-    lax.fori_loop(last, segments, unused, 0)
+    lax.fori_loop(last * SUB, segments, unused, 0)
     attended = []
     for g in range(heads // together):
         acc = acc_ref[g]
@@ -335,7 +344,7 @@
     back_ref,
     out_ref,
     x_ref,
-    grad_ref,
+    both_ref,
     gate_buf,
     up_buf,
     back_buf,
@@ -349,44 +358,50 @@
     shards = weight_ref.shape[0]
     rows = gate_buf.shape[0] // shards
     ff = weight_ref.shape[2]
-    others = [pltpu.make_async_copy(back_ref, back_buf, back_sem)]
-    for s in range(shards):
-        for i, buf in enumerate((gate_buf, up_buf)):
-            others.append(
-                pltpu.make_async_copy(
-                    weight_ref.at[s, pl.ds(i * rows, rows)],
-                    buf.at[pl.ds(s * rows, rows)],
-                    weight_sem.at[s, i],
-                )
+    gate_copies, up_copies = [
+        [
+            pltpu.make_async_copy(
+                weight_ref.at[s, pl.ds(i * rows, rows)],
+                buf.at[pl.ds(s * rows, rows)],
+                weight_sem.at[s, i],
             )
-    for copy in others:
+            for s in range(shards)
+        ]
+        for i, buf in enumerate((gate_buf, up_buf))
+    ]
+    back_copy = pltpu.make_async_copy(back_ref, back_buf, back_sem)
+    for copy in gate_copies + up_copies + [back_copy]:
         copy.start()
     unfold_rows(
         lambda f, n: row_ref[f : f + n, :], slots, chunks, unfold_matrix(BLOCK, chunks), x_ref
     )
     x = x_ref[...]
-    for copy in others:
-        copy.wait()
     step = 256
     gate_sum = jnp.zeros((slots, 1), F32)
     for j in range(ff // step):
         at = slice(j * step, (j + 1) * step)
-        w_gate, w_up = gate_buf[:, at], up_buf[:, at]
+        if j == 0:
+            for copy in gate_copies:
+                copy.wait()
+        gate_lin = dot(x, gate_buf[:, at])
+        if j == 0:
+            for copy in up_copies:
+                copy.wait()
+        up_lin = dot(x, up_buf[:, at])
+        if j == 0:
+            back_copy.wait()
         back = back_buf[:, at]
-        gate_lin = dot(x, w_gate)
-        up_lin = dot(x, w_up)
         sig = 0.5 * jnp.tanh(0.5 * gate_lin) + 0.5
         swish = gate_lin * sig
         up_back = back * swish
         gate_sum = gate_sum + jnp.sum(up_back * up_lin, axis=1, keepdims=True)
         gate_back = back * up_lin * (sig + swish * (1.0 - sig))
-        part = dot(gate_back.astype(BF16), w_gate, ((1,), (1,))) + dot(
-            up_back.astype(BF16), w_up, ((1,), (1,))
-        )
-        if j == 0:
-            grad_ref[...] = part
-        else:
-            grad_ref[...] += part
+        both_ref[:, at] = gate_back.astype(BF16)
+        both_ref[:, ff + j * step : ff + (j + 1) * step] = up_back.astype(BF16)
+    both = both_ref[...]
+    for n in range(0, width, step):
+        w = jnp.concatenate([gate_buf[n : n + step, :], up_buf[n : n + step, :]], axis=1)
+        x_ref[:, n : n + step] = dot(both, w, ((1,), (1,))).astype(BF16)
     experts = slots // capacity
     each = capacity * chunks
 
@@ -399,7 +414,7 @@
             out_ref[e, r : r + n, :] = rows[at - first : at - first + n, :]
             at += n
 
-    fold_rows(grad_ref[...].astype(BF16), fold_matrix(BLOCK, chunks), store)
+    fold_rows(x_ref[...], fold_matrix(BLOCK, chunks), store)
     high = gate_sum.astype(BF16)
     low = (gate_sum - high.astype(F32)).astype(BF16)
     slot, lane = iota((slots, LANES), 0), iota((slots, LANES), 1)
@@ -453,6 +468,7 @@
 
 HBM = pl.BlockSpec(memory_space=pltpu.HBM)
 TOGETHER = 8
+SUB = 4
 
 
 def attend(place, lens, kv, queries, hidden, proj, slot_table, *, rows, slots):
@@ -497,7 +513,7 @@
         out_specs=vmem(1)[0],
         scratch_shapes=[
             pltpu.VMEM((slots, width), BF16),
-            pltpu.VMEM((slots, width), F32),
+            pltpu.VMEM((slots, 2 * ff), BF16),
             pltpu.VMEM((width, ff), BF16),
             pltpu.VMEM((width, ff), BF16),
             pltpu.VMEM(back.shape, F32),

time: 196 us -> 190 us (0.969)
  the two profiles are of different devices: /device:TPU:22 before, /device:TPU:20 now
where the time goes in v5:
time: 190 us; the launch traced here: 189 us
  waiting for transfers between devices  66.7 us (35%)
  blocking collectives  44.9 us (24%)
  Pallas kernels  29.7 us (16%)
  starting transfers between devices  28.6 us (15%)
  between operations  14.2 us (7%)
  local copies, waits for them, and re-layouts  3.56 us (2%)
    all_to_all x1, blocking collectives, exchange(): return lax.all_to_all(rows, 'exp', split_axis=0, concat_axis=0, tiled=True)  44.9 us
    all_to_all x3, waiting for transfers between devices, exchange(): return lax.all_to_all(rows, 'exp', split_axis=0, concat_axis=0, tiled=True)  32.8 us
    all_to_all x3, starting transfers between devices, exchange(): return lax.all_to_all(rows, 'exp', split_axis=0, concat_axis=0, tiled=True)  28.5 us
    all_gather x1, waiting for transfers between devices, local(): weights = lax.all_gather(shard, 'seq', axis=0, tiled=False)  16.8 us
    all_gather x1, waiting for transfers between devices, local(): kv_all = lax.all_gather(segment, 'seq', axis=0, tiled=True)  16.4 us
    pallas_call x1, Pallas kernels, attend(): pl.pallas_call(functools.partial(attend_kernel, segments=segments, rows=r...  11.7 us
    pallas_call x1, Pallas kernels, expert(): pl.pallas_call(functools.partial(expert_kernel, capacity=capacity), out_s...  7.99 us
  transfers between devices with their start and end apart: 5, of which 5 were waited for; matrix products, arithmetic and copies ran while one was open for 2% of the time, Pallas kernels for 9%

profile of v5, /device:TPU:20, one launch (start us, length us, event | category | flops | bytes accessed | tf_op | source)
XLA Modules:
  0.0 189.1 jit_solution(11767124529195266040)
XLA Ops:
  7.2 0.0 copy-start.8
  7.2 2.3 %pack.1 = bf16[64,8,384]{2,1,0:T(8,128)(2,1)} custom-call(s32[4]{0:T(128)} %lens_ref.3, bf16[8,128]{1,0:T(8,128)(2,1)} %key_hbm.1, bf16[8,128]{1,0:T(8,128)(2,1)} %value_hbm.1), custom_call_target="tpu_custom_call" | custom-call | tf_op jit(solution)/shard_map/pack/pallas_call | solution.py:560
  9.5 16.5 %all-to-all-start = ((bf16[64,8,384]{2,1,0:T(8,128)(2,1)}), bf16[64,8,384]{2,1,0:T(8,128)(2,1)S(1)}, u32[]{:S(2)}, u32[]{:S(2)}) async-start(bf16[64,8,384]{2,1,0:T(8,128)(2,1)} %pack.1), calls=%async_computation | async-start | bytes 786432 | tf_op jit(solution)/shard_map/all_to_all | solution.py:529
  26.0 0.0 all-gather.4.cloned.1.call-start
  26.1 0.8 bitcast_dynamic-update-slice_fusion.5
  26.8 0.8 bitcast_dynamic-update-slice_fusion.4
  27.6 0.0 copy-done.1
  27.6 0.0 copy-done.5
  27.6 0.0 copy-done.4
  27.7 2.1 %dispatch.1 = (s32[8,128]{1,0:T(8,128)S(1)}, bf16[5120,128]{1,0:T(8,128)(2,1)}) custom-call(s32[4,128]{1,0:T(4,128)S(1)} %bitcast.33, bf16[4,128]{1,0:T(4,128)(2,1)S(1)} %bitcast.35, bf16[128,1024]{1,0:T(8,128)(2,1)S(1)} %copy-done.1), custom_call_target="tpu_custom_call" | custom-call | tf_op jit(solution)/shard_map/dispatch/pallas_call | solution.py:575
  29.8 0.6 copy-done.2
  30.4 0.9 pad_maximum_fusion
  31.3 11.4 %all-to-all-done = bf16[64,8,384]{2,1,0:T(8,128)(2,1)S(1)} async-done(((bf16[64,8,384]{2,1,0:T(8,128)(2,1)}), bf16[64,8,384]{2,1,0:T(8,128)(2,1)S(1)}, u32[]{:S(2)}, u32[]{:S(2)}) %all-to-all-start) | async-done | bytes 393248 | tf_op jit(solution)/shard_map/all_to_all | solution.py:529
  42.7 0.9 segment.1
  43.5 0.0 all-gather.4.cloned.1.call-update
  43.5 0.0 all-gather.6.cloned.1.call-start
  43.6 0.7 all-gather.6.cloned.1.call-update
  44.3 5.2 %all-to-all-start.1 = ((bf16[64,80,128]{2,1,0:T(8,128)(2,1)}), bf16[64,80,128]{2,1,0:T(8,128)(2,1)S(1)}, u32[]{:S(2)}, u32[]{:S(2)}) async-start(bf16[64,80,128]{2,1,0:T(8,128)(2,1)} %bitcast.14), calls=%async_computation.1 | async-start | bytes 2621440 | tf_op jit(solution)/shard_map/all_to_all | solution.py:529
  49.5 0.6 pad_add_fusion.place_ref
  50.1 16.4 %all-gather.4.cloned.1.call-done = bf16[4224,256]{1,0:T(8,128)(2,1)} async-done(((bf16[528,256]{1,0:T(8,128)(2,1)}), bf16[4224,256]{1,0:T(8,128)(2,1)}) %all-gather.4.cloned.1.call-update) | async-done | bytes 2162704 | tf_op jit(solution)/shard_map/all_gather | solution.py:600
  66.5 11.7 %attend.1 = bf16[5120,128]{1,0:T(8,128)(2,1)} custom-call(s32[2]{0:T(128)} %pad_add_fusion.place_ref, s32[4]{0:T(128)} %lens_ref.3, bf16[8,528,256]{2,1,0:T(8,128)(2,1)} %bitcast.40, bf16[128,1024]{1,0:T(8,128)(2,1)} %query_hbm.1, bf16[128,1024]{1,0:T(8,128)(2,1)} %hidden_hbm.1, bf16[1024,1024]{1,0:T(8,128)(2,1)} %proj_hbm.1, s32[8,128]{1,0:T(8,128)} %copy-done.2), custom_call_target="tpu_custom_call" | custom-call | tf_op jit(solution)/shard_map/attend/pallas_call | solution.py:479
  78.2 6.5 %all-to-all-done.1 = bf16[64,80,128]{2,1,0:T(8,128)(2,1)S(1)} async-done(((bf16[64,80,128]{2,1,0:T(8,128)(2,1)}), bf16[64,80,128]{2,1,0:T(8,128)(2,1)S(1)}, u32[]{:S(2)}, u32[]{:S(2)}) %all-to-all-start.1) | async-done | bytes 1310752 | tf_op jit(solution)/shard_map/all_to_all | solution.py:529
  84.7 6.8 %all-to-all-start.2 = ((bf16[64,80,128]{2,1,0:T(8,128)(2,1)}), bf16[64,80,128]{2,1,0:T(8,128)(2,1)S(1)}, u32[]{:S(2)}, u32[]{:S(2)}) async-start(bf16[64,80,128]{2,1,0:T(8,128)(2,1)} %bitcast.37), calls=%async_computation.2 | async-start | bytes 2621440 | tf_op jit(solution)/shard_map/all_to_all | solution.py:529
  91.6 16.8 %all-gather.6.cloned.1.call-done = bf16[3072,768]{1,0:T(8,128)(2,1)} async-done(((bf16[384,768]{1,0:T(8,128)(2,1)}), bf16[3072,768]{1,0:T(8,128)(2,1)}) %all-gather.6.cloned.1.call-update) | async-done | bytes 4718608 | tf_op jit(solution)/shard_map/all_gather | solution.py:602
  108.4 3.1 %prepare.1.back_ref = f32[640,768]{1,0:T(8,128)S(1)} custom-call(bf16[5120,128]{1,0:T(8,128)(2,1)S(1)} %bitcast.31, bf16[8,384,768]{2,1,0:T(8,128)(2,1)} %bitcast.38), custom_call_target="tpu_custom_call" | custom-call | flops 20132659200 | tf_op jit(solution)/shard_map/prepare/pallas_call | solution.py:617
  111.5 1.3 copy-done
  112.8 14.9 %all-to-all-done.2 = bf16[64,80,128]{2,1,0:T(8,128)(2,1)S(1)} async-done(((bf16[64,80,128]{2,1,0:T(8,128)(2,1)}), bf16[64,80,128]{2,1,0:T(8,128)(2,1)S(1)}, u32[]{:S(2)}, u32[]{:S(2)}) %all-to-all-start.2) | async-done | bytes 1310752 | tf_op jit(solution)/shard_map/all_to_all | solution.py:529
  127.7 8.0 %expert.1 = bf16[64,88,128]{2,1,0:T(8,128)(2,1)S(1)} custom-call(bf16[5120,128]{1,0:T(8,128)(2,1)S(1)} %bitcast.29, bf16[8,384,768]{2,1,0:T(8,128)(2,1)} %bitcast.39, f32[640,768]{1,0:T(8,128)} %copy-done), custom_call_target="tpu_custom_call" | custom-call | tf_op jit(solution)/shard_map/expert/pallas_call | solution.py:509
  135.7 0.0 copy-start.3
  135.7 44.9 %all_to_all.20.back_ref = bf16[64,88,128]{2,1,0:T(8,128)(2,1)S(1)} all-to-all(bf16[64,88,128]{2,1,0:T(8,128)(2,1)S(1)} %expert.1), channel_id=1, replica_groups=mesh['seq'=8,'exp'=64] {'exp'}, dimensions={0} | all-to-all | bytes 2883584 | tf_op jit(solution)/shard_map/all_to_all | solution.py:529
  180.6 0.0 copy-done.3
  180.6 1.7 combine.1
  (16 shorter events, 0.1 us)
Async XLA Ops:
  7.2 20.4 %copy-start.8 = (bf16[1,768,128]{2,1,0:T(8,128)(2,1)S(1)}, bf16[1,768,128]{2,1,0:T(8,128)(2,1)}, u32[]{:S(2)}) copy-start(bf16[1,768,128]{2,1,0:T(8,128)(2,1)} %param.22) | copy-start | bytes 589828
  7.2 20.5 %copy-start.1 = (bf16[128,1024]{1,0:T(8,128)(2,1)S(1)}, bf16[128,1024]{1,0:T(8,128)(2,1)}, u32[]{:S(2)}) copy-start(bf16[128,1024]{1,0:T(8,128)(2,1)} %cot_ref.1) | copy-start | bytes 786436
  7.2 20.5 %copy-start.5 = (bf16[128,4]{0,1:T(4,128)(2,1)S(1)}, bf16[128,4]{0,1:T(4,128)(2,1)}, u32[]{:S(2)}) copy-start(bf16[128,4]{0,1:T(4,128)(2,1)} %param.19) | copy-start | bytes 3076
  7.2 20.5 %copy-start.4 = (s32[128,4]{0,1:T(4,128)S(1)}, s32[128,4]{0,1:T(4,128)}, u32[]{:S(2)}) copy-start(s32[128,4]{0,1:T(4,128)} %param.18) | copy-start | bytes 6148
  7.2 23.2 %copy-start.6 = (bf16[1,128,768]{2,1,0:T(8,128)(2,1)S(1)}, bf16[1,128,768]{2,1,0:T(8,128)(2,1)}, u32[]{:S(2)}) copy-start(bf16[1,128,768]{2,1,0:T(8,128)(2,1)} %param.21) | copy-start | bytes 589828
  7.2 23.2 %copy-start.7 = (bf16[1,128,768]{2,1,0:T(8,128)(2,1)S(1)}, bf16[1,128,768]{2,1,0:T(8,128)(2,1)}, u32[]{:S(2)}) copy-start(bf16[1,128,768]{2,1,0:T(8,128)(2,1)} %param.20) | copy-start | bytes 589828
  9.5 33.1 %all-to-all-start = ((bf16[64,8,384]{2,1,0:T(8,128)(2,1)}), bf16[64,8,384]{2,1,0:T(8,128)(2,1)S(1)}, u32[]{:S(2)}, u32[]{:S(2)}) async-start(bf16[64,8,384]{2,1,0:T(8,128)(2,1)} %pack.1), calls=%async_computation | async-start | bytes 786432 | tf_op jit(solution)/shard_map/all_to_all | solution.py:529
  26.0 40.5 %all-gather.4.cloned.1.call-start = ((), (), s32[]{:S(2)}) async-start(), calls=%async_computation.4 | async-start | bytes 2433024 | tf_op jit(solution)/shard_map/all_gather | solution.py:600
  29.8 0.6 copy-start.2
  43.5 64.8 %all-gather.6.cloned.1.call-start = ((), (), s32[]{:S(2)}) async-start(), calls=%async_computation.5 | async-start | bytes 5308416 | tf_op jit(solution)/shard_map/all_gather | solution.py:602
  44.3 40.4 %all-to-all-start.1 = ((bf16[64,80,128]{2,1,0:T(8,128)(2,1)}), bf16[64,80,128]{2,1,0:T(8,128)(2,1)S(1)}, u32[]{:S(2)}, u32[]{:S(2)}) async-start(bf16[64,80,128]{2,1,0:T(8,128)(2,1)} %bitcast.14), calls=%async_computation.1 | async-start | bytes 2621440 | tf_op jit(solution)/shard_map/all_to_all | solution.py:529
  84.7 42.9 %all-to-all-start.2 = ((bf16[64,80,128]{2,1,0:T(8,128)(2,1)}), bf16[64,80,128]{2,1,0:T(8,128)(2,1)S(1)}, u32[]{:S(2)}, u32[]{:S(2)}) async-start(bf16[64,80,128]{2,1,0:T(8,128)(2,1)} %bitcast.37), calls=%async_computation.2 | async-start | bytes 2621440 | tf_op jit(solution)/shard_map/all_to_all | solution.py:529
  111.5 1.3 copy-start
  135.7 44.9 %copy-start.3 = (s32[8,128]{1,0:T(8,128)S(1)}, s32[8,128]{1,0:T(8,128)}, u32[]{:S(2)}) copy-start(s32[8,128]{1,0:T(8,128)} %copy-done.2) | copy-start | bytes 12292
Sparse Core Ops, SparseCore 0:
  43.7 22.7 all-gather.3
  68.6 39.7 all-gather.5

commit v6 on v5

--- a/solution.py
+++ b/solution.py
@@ -93,23 +93,32 @@
     total = lens_ref[0]
     for i in range(1, lens_ref.shape[0]):
         total = total + lens_ref[i]
-    rows = key_ref.shape[0]
-    tot = jnp.full((rows, LANES), total.astype(F32), F32).astype(BF16)
+    half = key_ref.shape[0] // 2
+    tot = jnp.full((half, LANES), total.astype(F32), F32)
     for copy in copies:
         copy.wait()
-    one = jnp.concatenate([key_ref[...], value_ref[...], tot], axis=1)
-    out_ref[...] = jnp.broadcast_to(one[None], (copies_out,) + one.shape)
-
-
-def segment_kernel(in_ref, out_ref, *, rows):
-    count = in_ref.shape[0]
-    out_ref[0:count, 0:LANES] = in_ref[:, 0:LANES]
+    key, value = key_ref[...].astype(F32), value_ref[...].astype(F32)
+    tiles = (key[:half], key[half:], value[:half], value[half:], tot)
+    for i, tile in enumerate(tiles):
+        out_ref[:, i] = jnp.broadcast_to(tile[None], (copies_out,) + tile.shape).astype(BF16)
+
+
+def segment_kernel(in_ref, out_ref):
+    sources, _, half, _ = in_ref.shape
+    count = sources * 2 * half
+
+    def whole(i):
+        parts = [in_ref[:, i].astype(F32), in_ref[:, i + 1].astype(F32)]
+        return jnp.concatenate(parts, axis=1).reshape(count, LANES)
+
+    keys, values = whole(0), whole(2)
+    out_ref[0:count, 0:LANES] = keys.astype(BF16)
     for i in range(0, count, LANES):
-        block = in_ref[i : i + LANES, LANES : 2 * LANES].astype(F32)
-        out_ref[i : i + LANES, LANES : 2 * LANES] = block.T.astype(BF16)
-    tot = in_ref[:, 2 * LANES :].astype(F32)
-    row, lane = iota(tot.shape, 0), iota(tot.shape, 1)
-    line = jnp.sum(jnp.where(row == lane * rows, tot, 0.0), axis=0, keepdims=True)
+        out_ref[i : i + LANES, LANES : 2 * LANES] = values[i : i + LANES, :].T.astype(BF16)
+    tot = in_ref[:, 4].astype(F32)
+    source, row, lane = iota(tot.shape, 0), iota(tot.shape, 1), iota(tot.shape, 2)
+    take = jnp.logical_and(row == 0, source == lane)
+    line = jnp.sum(jnp.sum(jnp.where(take, tot, 0.0), axis=0), axis=0, keepdims=True)
     more = out_ref.shape[0] - count
     line = jnp.broadcast_to(line, (more, LANES))
     out_ref[count:, :] = jnp.concatenate([line, jnp.zeros_like(line)], axis=1).astype(BF16)
@@ -559,7 +568,7 @@
 
     packed = pl.pallas_call(
         pack_kernel,
-        out_shape=jax.ShapeDtypeStruct((experts, own_rows, 3 * LANES), BF16),
+        out_shape=jax.ShapeDtypeStruct((experts, 5, own_rows // 2, LANES), BF16),
         in_specs=[SMEM, HBM, HBM],
         out_specs=vmem(1)[0],
         scratch_shapes=[
@@ -585,13 +594,13 @@
     )(ids, gates, cotangent)
 
     segment = pl.pallas_call(
-        functools.partial(segment_kernel, rows=own_rows),
+        segment_kernel,
         out_shape=jax.ShapeDtypeStruct((pitch, 2 * LANES), BF16),
         in_specs=vmem(1),
         out_specs=vmem(1)[0],
         compiler_params=params(16),
         name="segment",
-    )(kv_rows.reshape(rows, 3 * LANES))
+    )(kv_rows)
     lower = jnp.concatenate(
         [w_down[0][i * LANES : (i + 1) * LANES, :] for i in range(ff // LANES)], axis=1
     )

time: 190 us -> 191 us (level)
  waiting for transfers between devices: 66.7 us -> 61.1 us
  local copies, waits for them, and re-layouts: 3.56 us -> 7.93 us
    all_to_all x3, waiting for transfers between devices: 32.8 us -> 27.1 us  [exchange(): return lax.all_to_all(rows, 'exp', split_axis=0, concat_axis=0, tiled=True)]
    unnamed x24 -> x26, local copies, waits for them, and re-layouts: 3.53 us -> 7.14 us
  transfers between devices with their start and end apart: 5 -> 5, of which waited for: 5 -> 5; matrix products, arithmetic and copies ran while one was open for 2% -> 3% of each run, Pallas kernels for 9% -> 9%
where the time goes in v6:
time: 191 us; the launch traced here: 190 us
  waiting for transfers between devices  61.1 us (32%)
  blocking collectives  45.3 us (24%)
  starting transfers between devices  30.4 us (16%)
  Pallas kernels  29.7 us (16%)
  between operations  14.2 us (7%)
  local copies, waits for them, and re-layouts  7.93 us (4%)
    all_to_all x1, blocking collectives, exchange(): return lax.all_to_all(rows, 'exp', split_axis=0, concat_axis=0, tiled=True)  45.3 us
    all_to_all x3, starting transfers between devices, exchange(): return lax.all_to_all(rows, 'exp', split_axis=0, concat_axis=0, tiled=True)  30.3 us
    all_to_all x3, waiting for transfers between devices, exchange(): return lax.all_to_all(rows, 'exp', split_axis=0, concat_axis=0, tiled=True)  27.1 us
    all_gather x1, waiting for transfers between devices, local(): weights = lax.all_gather(shard, 'seq', axis=0, tiled=False)  16.8 us
    all_gather x1, waiting for transfers between devices, local(): kv_all = lax.all_gather(segment, 'seq', axis=0, tiled=True)  16.5 us
    pallas_call x1, Pallas kernels, attend(): pl.pallas_call(functools.partial(attend_kernel, segments=segments, rows=r...  11.7 us
    pallas_call x1, Pallas kernels, expert(): pl.pallas_call(functools.partial(expert_kernel, capacity=capacity), out_s...  7.99 us
    unnamed x26, local copies, waits for them, and re-layouts  7.14 us
  transfers between devices with their start and end apart: 5, of which 5 were waited for; matrix products, arithmetic and copies ran while one was open for 3% of the time, Pallas kernels for 9%

profile of v6, /device:TPU:20, one launch (start us, length us, event | category | flops | bytes accessed | tf_op | source)
XLA Modules:
  0.0 190.1 jit_solution(5466847464853575755)
XLA Ops:
  7.2 2.3 %pack.1 = bf16[64,5,4,128]{3,2,1,0:T(4,128)(2,1)} custom-call(s32[4]{0:T(128)} %lens_ref.3, bf16[8,128]{1,0:T(8,128)(2,1)} %key_hbm.1, bf16[8,128]{1,0:T(8,128)(2,1)} %value_hbm.1), custom_call_target="tpu_custom_call" | custom-call | tf_op jit(solution)/shard_map/pack/pallas_call | solution.py:569
  9.5 16.5 %all-to-all-start = ((bf16[64,5,4,128]{3,2,1,0:T(4,128)(2,1)}), bf16[64,5,4,128]{3,2,1,0:T(4,128)(2,1)S(1)}, u32[]{:S(2)}, u32[]{:S(2)}) async-start(bf16[64,5,4,128]{3,2,1,0:T(4,128)(2,1)} %pack.1), calls=%async_computation | async-start | bytes 655360 | tf_op jit(solution)/shard_map/all_to_all | solution.py:538
  26.0 0.0 all-gather.4.cloned.1.call-start
  26.1 0.8 bitcast_dynamic-update-slice_fusion.5
  26.8 0.8 bitcast_dynamic-update-slice_fusion.4
  27.6 0.8 bitcast_dynamic-update-slice_fusion.3
  28.4 0.8 bitcast_dynamic-update-slice_fusion.2
  29.2 0.7 copy-done.4
  29.8 0.7 copy-done.6
  30.5 2.1 %dispatch.1 = (s32[8,128]{1,0:T(8,128)S(1)}, bf16[5120,128]{1,0:T(8,128)(2,1)}) custom-call(s32[4,128]{1,0:T(4,128)S(1)} %bitcast.31, bf16[4,128]{1,0:T(4,128)(2,1)S(1)} %bitcast.33, bf16[128,1024]{1,0:T(8,128)(2,1)S(1)} %copy-done.1), custom_call_target="tpu_custom_call" | custom-call | tf_op jit(solution)/shard_map/dispatch/pallas_call | solution.py:584
  32.6 0.6 copy-done.2
  33.2 0.8 bitcast_dynamic-update-slice_fusion.1
  34.0 0.8 bitcast_dynamic-update-slice_fusion
  34.7 0.9 pad_maximum_fusion
  35.6 5.7 %all-to-all-done.in_ref = bf16[64,5,4,128]{3,2,1,0:T(4,128)(2,1)S(1)} async-done(((bf16[64,5,4,128]{3,2,1,0:T(4,128)(2,1)}), bf16[64,5,4,128]{3,2,1,0:T(4,128)(2,1)S(1)}, u32[]{:S(2)}, u32[]{:S(2)}) %all-to-all-start) | async-done | bytes 327712 | tf_op jit(solution)/shard_map/all_to_all | solution.py:538
  41.3 0.9 segment.1
  42.3 0.0 all-gather.4.cloned.1.call-update
  42.3 0.0 all-gather.6.cloned.1.call-start
  42.3 0.7 all-gather.6.cloned.1.call-update
  43.0 7.0 %all-to-all-start.1 = ((bf16[64,80,128]{2,1,0:T(8,128)(2,1)}), bf16[64,80,128]{2,1,0:T(8,128)(2,1)S(1)}, u32[]{:S(2)}, u32[]{:S(2)}) async-start(bf16[64,80,128]{2,1,0:T(8,128)(2,1)} %bitcast.13), calls=%async_computation.1 | async-start | bytes 2621440 | tf_op jit(solution)/shard_map/all_to_all | solution.py:538
  50.0 0.6 pad_add_fusion.place_ref
  50.6 16.5 %all-gather.4.cloned.1.call-done = bf16[4224,256]{1,0:T(8,128)(2,1)} async-done(((bf16[528,256]{1,0:T(8,128)(2,1)}), bf16[4224,256]{1,0:T(8,128)(2,1)}) %all-gather.4.cloned.1.call-update) | async-done | bytes 2162704 | tf_op jit(solution)/shard_map/all_gather | solution.py:609
  67.0 11.7 %attend.1 = bf16[5120,128]{1,0:T(8,128)(2,1)} custom-call(s32[2]{0:T(128)} %pad_add_fusion.place_ref, s32[4]{0:T(128)} %lens_ref.3, bf16[8,528,256]{2,1,0:T(8,128)(2,1)} %bitcast.38, bf16[128,1024]{1,0:T(8,128)(2,1)} %query_hbm.1, bf16[128,1024]{1,0:T(8,128)(2,1)} %hidden_hbm.1, bf16[1024,1024]{1,0:T(8,128)(2,1)} %proj_hbm.1, s32[8,128]{1,0:T(8,128)} %copy-done.2), custom_call_target="tpu_custom_call" | custom-call | tf_op jit(solution)/shard_map/attend/pallas_call | solution.py:488
  78.7 6.6 %all-to-all-done.1 = bf16[64,80,128]{2,1,0:T(8,128)(2,1)S(1)} async-done(((bf16[64,80,128]{2,1,0:T(8,128)(2,1)}), bf16[64,80,128]{2,1,0:T(8,128)(2,1)S(1)}, u32[]{:S(2)}, u32[]{:S(2)}) %all-to-all-start.1) | async-done | bytes 1310752 | tf_op jit(solution)/shard_map/all_to_all | solution.py:538
  85.3 6.8 %all-to-all-start.2 = ((bf16[64,80,128]{2,1,0:T(8,128)(2,1)}), bf16[64,80,128]{2,1,0:T(8,128)(2,1)S(1)}, u32[]{:S(2)}, u32[]{:S(2)}) async-start(bf16[64,80,128]{2,1,0:T(8,128)(2,1)} %bitcast.35), calls=%async_computation.2 | async-start | bytes 2621440 | tf_op jit(solution)/shard_map/all_to_all | solution.py:538
  92.1 16.8 %all-gather.6.cloned.1.call-done = bf16[3072,768]{1,0:T(8,128)(2,1)} async-done(((bf16[384,768]{1,0:T(8,128)(2,1)}), bf16[3072,768]{1,0:T(8,128)(2,1)}) %all-gather.6.cloned.1.call-update) | async-done | bytes 4718608 | tf_op jit(solution)/shard_map/all_gather | solution.py:611
  108.9 3.1 %prepare.1.back_ref = f32[640,768]{1,0:T(8,128)S(1)} custom-call(bf16[5120,128]{1,0:T(8,128)(2,1)S(1)} %bitcast.29, bf16[8,384,768]{2,1,0:T(8,128)(2,1)} %bitcast.36), custom_call_target="tpu_custom_call" | custom-call | flops 20132659200 | tf_op jit(solution)/shard_map/prepare/pallas_call | solution.py:626
  112.0 1.3 copy-done
  113.3 14.8 %all-to-all-done.2 = bf16[64,80,128]{2,1,0:T(8,128)(2,1)S(1)} async-done(((bf16[64,80,128]{2,1,0:T(8,128)(2,1)}), bf16[64,80,128]{2,1,0:T(8,128)(2,1)S(1)}, u32[]{:S(2)}, u32[]{:S(2)}) %all-to-all-start.2) | async-done | bytes 1310752 | tf_op jit(solution)/shard_map/all_to_all | solution.py:538
  128.2 8.0 %expert.1 = bf16[64,88,128]{2,1,0:T(8,128)(2,1)S(1)} custom-call(bf16[5120,128]{1,0:T(8,128)(2,1)S(1)} %bitcast.28, bf16[8,384,768]{2,1,0:T(8,128)(2,1)} %bitcast.37, f32[640,768]{1,0:T(8,128)} %copy-done), custom_call_target="tpu_custom_call" | custom-call | tf_op jit(solution)/shard_map/expert/pallas_call | solution.py:518
  136.2 45.3 %all_to_all.20.back_ref = bf16[64,88,128]{2,1,0:T(8,128)(2,1)S(1)} all-to-all(bf16[64,88,128]{2,1,0:T(8,128)(2,1)S(1)} %expert.1), channel_id=1, replica_groups=mesh['seq'=8,'exp'=64] {'exp'}, dimensions={0} | all-to-all | bytes 2883584 | tf_op jit(solution)/shard_map/all_to_all | solution.py:538
  181.6 1.6 combine.1
  (18 shorter events, 0.1 us)
Async XLA Ops:
  7.2 22.0 %copy-start.1 = (bf16[128,1024]{1,0:T(8,128)(2,1)S(1)}, bf16[128,1024]{1,0:T(8,128)(2,1)}, u32[]{:S(2)}) copy-start(bf16[128,1024]{1,0:T(8,128)(2,1)} %cot_ref.1) | copy-start | bytes 786436
  7.2 27.6 %copy-start.8 = (bf16[1,128,768]{2,1,0:T(8,128)(2,1)S(1)}, bf16[1,128,768]{2,1,0:T(8,128)(2,1)}, u32[]{:S(2)}) copy-start(bf16[1,128,768]{2,1,0:T(8,128)(2,1)} %param.21) | copy-start | bytes 589828
  7.2 27.5 %copy-start.9 = (bf16[1,128,768]{2,1,0:T(8,128)(2,1)S(1)}, bf16[1,128,768]{2,1,0:T(8,128)(2,1)}, u32[]{:S(2)}) copy-start(bf16[1,128,768]{2,1,0:T(8,128)(2,1)} %param.20) | copy-start | bytes 589828
  9.5 31.8 %all-to-all-start = ((bf16[64,5,4,128]{3,2,1,0:T(4,128)(2,1)}), bf16[64,5,4,128]{3,2,1,0:T(4,128)(2,1)S(1)}, u32[]{:S(2)}, u32[]{:S(2)}) async-start(bf16[64,5,4,128]{3,2,1,0:T(4,128)(2,1)} %pack.1), calls=%async_computation | async-start | bytes 655360 | tf_op jit(solution)/shard_map/all_to_all | solution.py:538
  26.0 41.0 %all-gather.4.cloned.1.call-start = ((), (), s32[]{:S(2)}) async-start(), calls=%async_computation.4 | async-start | bytes 2433024 | tf_op jit(solution)/shard_map/all_gather | solution.py:609
  29.1 0.7 copy-start.4
  29.8 0.7 copy-start.6
  32.6 0.6 copy-start.2
  42.3 66.6 %all-gather.6.cloned.1.call-start = ((), (), s32[]{:S(2)}) async-start(), calls=%async_computation.5 | async-start | bytes 5308416 | tf_op jit(solution)/shard_map/all_gather | solution.py:611
  43.0 42.3 %all-to-all-start.1 = ((bf16[64,80,128]{2,1,0:T(8,128)(2,1)}), bf16[64,80,128]{2,1,0:T(8,128)(2,1)S(1)}, u32[]{:S(2)}, u32[]{:S(2)}) async-start(bf16[64,80,128]{2,1,0:T(8,128)(2,1)} %bitcast.13), calls=%async_computation.1 | async-start | bytes 2621440 | tf_op jit(solution)/shard_map/all_to_all | solution.py:538
  85.3 42.9 %all-to-all-start.2 = ((bf16[64,80,128]{2,1,0:T(8,128)(2,1)}), bf16[64,80,128]{2,1,0:T(8,128)(2,1)S(1)}, u32[]{:S(2)}, u32[]{:S(2)}) async-start(bf16[64,80,128]{2,1,0:T(8,128)(2,1)} %bitcast.35), calls=%async_computation.2 | async-start | bytes 2621440 | tf_op jit(solution)/shard_map/all_to_all | solution.py:538
  112.0 1.3 copy-start
  136.2 45.4 %copy-start.3 = (s32[8,128]{1,0:T(8,128)S(1)}, s32[8,128]{1,0:T(8,128)}, u32[]{:S(2)}) copy-start(s32[8,128]{1,0:T(8,128)} %copy-done.2) | copy-start | bytes 12292
  136.2 45.4 %copy-start.5 = (s32[128,4]{0,1:T(4,128)S(1)}, s32[128,4]{0,1:T(4,128)}, u32[]{:S(2)}) copy-start(s32[128,4]{0,1:T(4,128)} %param.18) | copy-start | bytes 6148
  136.2 45.4 %copy-start.7 = (bf16[128,4]{0,1:T(4,128)(2,1)S(1)}, bf16[128,4]{0,1:T(4,128)(2,1)}, u32[]{:S(2)}) copy-start(bf16[128,4]{0,1:T(4,128)(2,1)} %param.19) | copy-start | bytes 3076
Sparse Core Ops, SparseCore 0:
  42.4 24.5 all-gather.3
  69.2 39.7 all-gather.5
